TPU v7x, 128 devices: a whole 4x4x4 slice. The times are simulated.
128 devices in a mesh: dp: 4 (over z), lat: 16 (over y, x_lo, core), lon: 2 (over x_hi).
Axes of the slice: x: 4 (x_hi: 2, x_lo: 2; x = x_hi * 2 + x_lo), y: 4, z: 4, core: 2. Of those that a mesh axis runs over, the one named last changes fastest.
Arguments:
- fields: bfloat16 [4, 384, 768, 384], P('dp', 'lat', 'lon'), may hold values from -6 to 6
- cotangent: bfloat16 [4, 384, 768, 384], P('dp', 'lat', 'lon'), may hold values from -6 to 6
- w_first: bfloat16 [4, 2, 96, 96], P('lon'), may hold values from -0.4375 to 0.4375
- w_second: bfloat16 [4, 2, 96, 96], P('lon'), may hold values from -0.4375 to 0.4375
- bias_first: float32 [4, 2, 96], P('lon'), may hold values from -3 to 3
Outputs:
- grad_fields: bfloat16 [4, 384, 768, 384], P('dp', 'lat', 'lon')
- grad_w_first: float32 [4, 2, 96, 96], P('lon')
- grad_w_second: float32 [4, 2, 96, 96], P('lon')
- grad_bias_first: float32 [4, 2, 96], P('lon')
All inputs are finite; a program needn't handle non-finite values.
Results may differ from a plain program's by a relative error of at most 0.012.
The roundings to bfloat16 on the way count: a program that leaves them out, or rounds other values in their place, can miss the bound.
Values may be sent and summed in bfloat16 or wider, within the bound.
A program may use at most 128 MiB of HBM per device.

v0:
```python
import math

import jax
import jax.numpy as jnp
from jax import lax
from jax.sharding import PartitionSpec as P

KW = 96


shrink_level = 0.05
gelu_coef = 0.044715


def smooth_act(value):
    inner = math.sqrt(2.0 / math.pi) * (value + gelu_coef * value * value * value)
    return 0.5 * value * (1.0 + jnp.tanh(inner))


def smooth_slope(value):
    root = math.sqrt(2.0 / math.pi)
    tangent = jnp.tanh(root * (value + gelu_coef * value * value * value))
    return 0.5 * (1.0 + tangent) + 0.5 * value * (1.0 - tangent * tangent) * root * (
        1.0 + 3.0 * gelu_coef * value * value
    )


def shrink_gate(value):
    square = value * value
    return square / (square + shrink_level * shrink_level)


def lon_table(wavenums, longitudes):
    kk = jnp.arange(wavenums, dtype=jnp.int32)[:, None]
    ww = jnp.arange(longitudes, dtype=jnp.int32)[None, :]
    phase = (kk * ww % longitudes).astype(jnp.float32) * (2.0 * math.pi / longitudes)
    return jnp.stack([jnp.cos(phase), -jnp.sin(phase)], 0).astype(jnp.bfloat16)


def lat_table(latitudes):
    pp = jnp.arange(latitudes, dtype=jnp.int32)[:, None]
    hh = jnp.arange(latitudes, dtype=jnp.int32)[None, :]
    phase = (pp * hh % latitudes).astype(jnp.float32) * (2.0 * math.pi / latitudes)
    cosine = jnp.cos(phase)
    sine = jnp.sin(phase)
    return jnp.stack([jnp.stack([cosine, sine], 0), jnp.stack([-sine, cosine], 0)], 0).astype(
        jnp.bfloat16
    )


def matmul_fwd(left, right):
    return jnp.einsum("nbi,bio->nbo", left, right, preferred_element_type=jnp.float32)


def matmul_adj(left, right):
    return jnp.einsum("nbo,bio->nbi", left, right, preferred_element_type=jnp.float32)


def matmul_grad(left, right):
    return jnp.einsum("nbi,nbo->bio", left, right, preferred_element_type=jnp.float32)


def complex_apply(zre, zim, weight):
    w_real = weight[:, 0]
    w_imag = weight[:, 1]
    return (
        matmul_fwd(zre, w_real) - matmul_fwd(zim, w_imag),
        matmul_fwd(zre, w_imag) + matmul_fwd(zim, w_real),
    )


def complex_adjoint(dre, dim, weight):
    w_real = weight[:, 0]
    w_imag = weight[:, 1]
    return (
        matmul_adj(dre, w_real) + matmul_adj(dim, w_imag),
        matmul_adj(dim, w_real) - matmul_adj(dre, w_imag),
    )


def complex_grad(zre, zim, dre, dim):
    real = matmul_grad(zre, dre) + matmul_grad(zim, dim)
    imag = matmul_grad(zre, dim) - matmul_grad(zim, dre)
    return jnp.stack([real, imag], 1)


def on_device(fields, cotangent, w_first, w_second, bias_first):
    samples, lat_rows, lon_cols, channels = fields.shape
    longitudes = lon_cols * lax.axis_size("lon")
    latitudes = lat_rows * lax.axis_size("lat")
    lon_norm = 1.0 / math.sqrt(longitudes)
    lat_norm = 1.0 / math.sqrt(latitudes)
    table_w = lon_table(KW, longitudes)
    table_h = lat_table(latitudes)
    blocks = w_first.shape[0]
    block_size = w_first.shape[2]
    local_channels = blocks * block_size
    cells, cot_cells = (
        lax.all_to_all(fields, "lon", split_axis=3, concat_axis=2, tiled=True),
        lax.all_to_all(cotangent, "lon", split_axis=3, concat_axis=2, tiled=True),
    )
    spec_a = (
        jnp.einsum("rkw,shwc->shrkc", table_w, cells, preferred_element_type=jnp.float32) * lon_norm
    ).astype(jnp.bfloat16)
    spec_g = (
        jnp.einsum("rkw,shwc->shrkc", table_w, cot_cells, preferred_element_type=jnp.float32)
        * lon_norm
    ).astype(jnp.bfloat16)

    def lat_transform(spectrum):
        return (
            jnp.einsum("qrph,shrkc->sqpkc", table_h, spectrum, preferred_element_type=jnp.float32)
            * lat_norm
        )

    field_cols, cot_cols = (
        lax.all_to_all(spec_a, "lat", split_axis=3, concat_axis=1, tiled=True),
        lax.all_to_all(spec_g, "lat", split_axis=3, concat_axis=1, tiled=True),
    )
    freq = lat_transform(field_cols).astype(jnp.bfloat16)
    freq_re = freq[:, 0].reshape(-1, blocks, block_size)
    freq_im = freq[:, 1].reshape(-1, blocks, block_size)
    o1re, o1im = complex_apply(freq_re, freq_im, w_first)
    o1re = o1re + bias_first[:, 0]
    o1im = o1im + bias_first[:, 1]
    h1re = smooth_act(o1re).astype(jnp.bfloat16)
    h1im = smooth_act(o1im).astype(jnp.bfloat16)
    o2re, o2im = complex_apply(h1re, h1im, w_second)
    freq_re, freq_im, o1re, o1im, h1re, h1im, keep_re, keep_im = (
        freq_re,
        freq_im,
        o1re,
        o1im,
        h1re,
        h1im,
        shrink_gate(o2re),
        shrink_gate(o2im),
    )
    wave_here = cot_cols.shape[3]
    wave_index = lax.axis_index("lat") * wave_here + jnp.arange(wave_here, dtype=jnp.int32)
    doubling = jnp.where(wave_index == 0, 1.0, 2.0).astype(jnp.float32)[None, None, :, None]
    gfreq = lat_transform(cot_cols)
    dre = (keep_re * (gfreq[:, 0] * doubling).reshape(-1, blocks, block_size)).astype(jnp.bfloat16)
    dim = (keep_im * (gfreq[:, 1] * doubling).reshape(-1, blocks, block_size)).astype(jnp.bfloat16)
    dhre, dhim = complex_adjoint(dre, dim, w_second)
    dzre = (smooth_slope(o1re) * dhre).astype(jnp.bfloat16)
    dzim = (smooth_slope(o1im) * dhim).astype(jnp.bfloat16)
    grad_two = complex_grad(h1re, h1im, dre, dim)
    grad_one = complex_grad(freq_re, freq_im, dzre, dzim)
    grad_bias = jnp.stack(
        [jnp.sum(dzre.astype(jnp.float32), 0), jnp.sum(dzim.astype(jnp.float32), 0)], 1
    )
    spec_rows = samples * lax.axis_size("dp") * latitudes * KW
    scale = 1.0 / math.sqrt(spec_rows)
    dsre, dsim = complex_adjoint(dzre, dzim, w_first)
    col_shape = (samples, latitudes, wave_here, local_channels)
    dspec = jnp.stack([dsre.reshape(col_shape), dsim.reshape(col_shape)], 1).astype(jnp.bfloat16)
    back = (
        jnp.einsum("qrph,sqpkc->shrkc", table_h, dspec, preferred_element_type=jnp.float32)
        * lat_norm
    ).astype(jnp.bfloat16)
    rows_back = lax.all_to_all(back, "lat", split_axis=1, concat_axis=3, tiled=True)
    grad_one, grad_two, grad_bias = lax.psum(
        (grad_one * scale, grad_two * scale, grad_bias * scale), ("dp", "lat")
    )
    spatial = (
        jnp.einsum("rkw,shrkc->shwc", table_w, rows_back, preferred_element_type=jnp.float32)
        * lon_norm
    )
    grad_cells = (cot_cells.astype(jnp.float32) + spatial).astype(jnp.bfloat16)
    grad_fields = lax.all_to_all(grad_cells, "lon", split_axis=2, concat_axis=3, tiled=True)
    return (grad_fields, grad_one, grad_two, grad_bias)


def solution(mesh):
    placed = (
        P("dp", "lat", "lon", None),
        P("dp", "lat", "lon", None),
        P("lon", None, None, None),
        P("lon", None, None, None),
        P("lon", None, None),
    )
    return jax.shard_map(
        on_device,
        mesh=mesh,
        in_specs=placed,
        out_specs=(
            P("dp", "lat", "lon", None),
            P("lon", None, None, None),
            P("lon", None, None, None),
            P("lon", None, None),
        ),
        check_vma=False,
    )
```

profile of v0, /device:TPU:1, one launch (start us, length us, event | category | flops | bytes accessed | tf_op | source)
XLA Modules:
  0.0 1022.6 jit_solution(10042687327155879825)
XLA Ops:
  7.2 10.2 %copy.138 = bf16[1,24,384,384]{2,1,0,3:T(8,128)(2,1)} copy(bf16[1,24,384,384]{3,2,1,0:T(8,128)(2,1)} %param.5) | data formatting | bytes 14155776 | tf_op args[0]
  17.4 6.6 all-to-all-start.1
  24.1 10.2 copy.135
  34.2 69.4 %all-to-all-done.1 = bf16[1,24,384,384]{2,1,0,3:T(8,128)(2,1)} async-done(((bf16[1,24,384,384]{2,1,0,3:T(8,128)(2,1)}), bf16[1,24,384,384]{2,1,0,3:T(8,128)(2,1)}, u32[]{:S(2)}, u32[]{:S(2)}) %all-to-all-start.1) | async-done | bytes 7077920 | tf_op jit(solution)/shard_map/all_to_all | solution.py:99
  103.6 6.5 all-to-all-start
  111.5 4.4 copy.139
  115.8 22.1 %copy.140 = bf16[1,24,2,384,192]{3,2,4,1,0:T(2,128)(2,1)} copy(bf16[1,24,2,384,192]{3,4,2,1,0:T(8,128)(2,1)S(1)} %bitcast.259) | data formatting | bytes 14155776 | tf_op jit(solution)/shard_map/all_to_all | solution.py:99
  137.9 16.1 %reshape.228 = bf16[24,768,192,1]{1,2,0,3:T(8,128)(2,1)} reshape(bf16[1,24,2,384,192]{3,2,4,1,0:T(2,128)(2,1)} %copy.140) | data formatting | bytes 14155776 | tf_op jit(solution)/shard_map/reshape
  154.0 5.0 fusion.26
  159.1 2.7 copy.141
  161.8 26.4 %all-to-all-done = bf16[1,24,384,384]{2,1,0,3:T(8,128)(2,1)} async-done(((bf16[1,24,384,384]{2,1,0,3:T(8,128)(2,1)}), bf16[1,24,384,384]{2,1,0,3:T(8,128)(2,1)}, u32[]{:S(2)}, u32[]{:S(2)}) %all-to-all-start) | async-done | bytes 7077920 | tf_op jit(solution)/shard_map/all_to_all | solution.py:100
  188.2 9.1 all-to-all-start.2
  197.5 2.3 fusion.64
  199.8 2.6 negate_convert_fusion
  203.4 4.5 copy.136
  207.9 3.0 copy-done
  210.8 21.9 %copy.155 = bf16[1,24,2,384,192]{3,2,4,1,0:T(2,128)(2,1)} copy(bf16[1,24,2,384,192]{3,4,2,1,0:T(8,128)(2,1)S(1)} %bitcast.256) | data formatting | bytes 14155776 | tf_op jit(solution)/shard_map/all_to_all | solution.py:100
  232.7 16.1 %reshape.232 = bf16[24,768,192,1]{1,2,0,3:T(8,128)(2,1)} reshape(bf16[1,24,2,384,192]{3,2,4,1,0:T(2,128)(2,1)} %copy.155) | data formatting | bytes 14155776 | tf_op jit(solution)/shard_map/reshape.6
  248.9 5.0 fusion.27
  253.9 2.8 copy.156
  256.7 6.0 all-to-all-start.3
  263.9 2.2 fusion.45
  269.6 1.7 copy.147
  271.3 2.2 copy.148
  273.5 1.8 reshape_squeeze.7
  275.3 2.7 copy.150
  280.1 2.1 multiply_convert_fusion.3
  282.2 1.7 fusion.84
  283.9 1.7 fusion.76
  285.6 7.0 all-to-all-done.3
  292.6 1.8 copy.157
  295.5 2.2 fusion.20
  297.6 2.0 fusion.118
  299.7 3.4 copy.160
  303.1 4.7 squeeze.26
  307.8 4.3 copy.161
  312.2 3.8 multiply_convert_fusion.2
  319.3 3.4 copy.163
  322.7 4.7 squeeze.27
  327.4 4.1 copy.164
  331.6 2.8 fusion.23
  343.8 3.7 copy.170
  347.5 4.1 stack.70
  351.6 2.6 copy.174
  354.2 2.9 fusion.17
  357.0 3.7 copy.173
  360.7 4.1 stack.71
  364.8 2.8 copy.175
  367.6 4.6 fusion.50
  372.2 6.8 copy.177
  379.0 5.0 all-to-all-start.4
  384.0 9.9 convert_bitcast_fusion
  393.9 11.3 %copy.216 = f32[1,24,2,24,8,384]{5,4,2,3,1,0:T(8,128)} copy(f32[1,24,2,24,8,384]{5,4,3,2,1,0:T(8,128)} %convert_bitcast_fusion) | data formatting | bytes 28311552 | tf_op jit(solution)/shard_map/convert_element_type | solution.py:170
  405.2 8.9 all-to-all-done.4
  414.1 2.0 copy.178
  417.1 8.3 fusion
  425.5 13.4 %copy.181 = bf16[1,24,768,192]{3,1,0,2:T(8,128)(2,1)} copy(bf16[1,24,768,192]{2,3,1,0:T(8,128)(2,1)} %fusion) | data formatting | bytes 14155776 | tf_op jit(solution)/shard_map/convert_element_type | solution.py:170
  438.9 7.3 all-to-all-start.5
  446.3 1.7 fusion.123
  452.5 231.2 %psum.23 = f32[2,2,96]{2,1,0:T(2,128)} all-reduce(f32[2,2,96]{2,1,0:T(2,128)S(1)} %maximum_multiply_fusion.2), channel_id=1, replica_groups=mesh['dp'=4,'lat'=16,'lon'=2] {'dp','lat'}, use_global_device_ids=true, to_apply=%region_4.5 | all-reduce | flops 384 | bytes 3072 | tf_op jit(solution)/shard_map/psum | solution.py:163
  683.7 293.6 %all-reduce.3.cloned.1.call-done = (f32[2,2,96,96]{3,2,0,1:T(8,128)}, f32[2,2,96,96]{3,2,0,1:T(8,128)}) async-done(((f32[2,2,96,96]{3,2,0,1:T(8,128)}, f32[2,2,96,96]{3,2,0,1:T(8,128)}), (f32[2,2,96,96]{3,2,0,1:T(8,128)}, f32[2,2,96,96]{3,2,0,1:T(8,128)})) %all-reduce.3.cloned.1.call-update) | async-done | bytes 294928 | tf_op jit(solution)/shard_map/psum | solution.py:163
  980.6 17.0 %copy.211 = bf16[1,24,2,384,192]{3,2,4,1,0:T(2,128)(2,1)} copy(bf16[1,24,2,384,192]{4,1,3,2,0:T(8,128)(2,1)} %bitcast.63) | data formatting | bytes 14155776 | tf_op jit(solution)/shard_map/all_to_all | solution.py:171
  997.6 7.4 copy.183
  1005.0 10.3 %copy.188 = bf16[1,24,384,384]{3,2,1,0:T(8,128)(2,1)} copy(bf16[1,24,384,384]{2,3,1,0:T(8,128)(2,1)} %bitcast.260) | data formatting | bytes 14155776
  (94 shorter events, 31.6 us)
Async XLA Ops:
  17.4 86.2 %all-to-all-start.1 = ((bf16[1,24,384,384]{2,1,0,3:T(8,128)(2,1)}), bf16[1,24,384,384]{2,1,0,3:T(8,128)(2,1)}, u32[]{:S(2)}, u32[]{:S(2)}) async-start(bf16[1,24,384,384]{2,1,0,3:T(8,128)(2,1)} %copy.138), calls=%async_computation.1 | async-start | bytes 14155776 | tf_op jit(solution)/shard_map/all_to_all | solution.py:99
  103.6 84.6 %all-to-all-start = ((bf16[1,24,384,384]{2,1,0,3:T(8,128)(2,1)}), bf16[1,24,384,384]{2,1,0,3:T(8,128)(2,1)}, u32[]{:S(2)}, u32[]{:S(2)}) async-start(bf16[1,24,384,384]{2,1,0,3:T(8,128)(2,1)} %copy.135), calls=%async_computation | async-start | bytes 14155776 | tf_op jit(solution)/shard_map/all_to_all | solution.py:100
  111.4 137.5 %copy-start.20 = (bf16[1,96,768]{2,1,0:T(8,128)(2,1)}, bf16[1,96,768]{2,1,0:T(8,128)(2,1)S(1)}, u32[]{:S(2)}) copy-start(bf16[1,96,768]{2,1,0:T(8,128)(2,1)S(1)} %get-tuple-element.38) | copy-start | bytes 442372
  111.4 137.4 %copy-start.22 = (bf16[1,96,768]{2,1,0:T(8,128)(2,1)}, bf16[1,96,768]{2,1,0:T(8,128)(2,1)S(1)}, u32[]{:S(2)}) copy-start(bf16[1,96,768]{2,1,0:T(8,128)(2,1)S(1)} %get-tuple-element.39) | copy-start | bytes 442372
  188.2 68.4 %all-to-all-start.2 = ((bf16[1,24,2,96,192]{4,1,2,0,3:T(8,128)(2,1)}), bf16[1,24,2,96,192]{4,1,2,0,3:T(8,128)(2,1)S(1)}, u32[]{:S(2)}, u32[]{:S(2)}) async-start(bf16[1,24,2,96,192]{4,1,2,0,3:T(8,128)(2,1)} %copy.141), calls=%async_computation.2 | async-start | bytes 4718592 | tf_op jit(solution)/shard_map/all_to_all | solution.py:117
  197.3 6.1 copy-start.27
  203.4 91.3 %copy-start.17 = (bf16[1,2,384,384]{3,2,1,0:T(8,128)(2,1)}, bf16[1,2,384,384]{3,2,1,0:T(8,128)(2,1)S(1)}, u32[]{:S(2)}) copy-start(bf16[1,2,384,384]{3,2,1,0:T(8,128)(2,1)S(1)} %get-tuple-element.26) | copy-start | bytes 1769476
  207.9 3.0 copy-start
  256.7 35.9 %all-to-all-start.3 = ((bf16[1,24,2,96,192]{4,1,2,0,3:T(8,128)(2,1)}), bf16[1,24,2,96,192]{4,1,2,0,3:T(8,128)(2,1)}, u32[]{:S(2)}, u32[]{:S(2)}) async-start(bf16[1,24,2,96,192]{4,1,2,0,3:T(8,128)(2,1)} %copy.156), calls=%async_computation.3 | async-start | bytes 4718592 | tf_op jit(solution)/shard_map/all_to_all | solution.py:118
  262.9 1.1 copy-start.18
  273.5 4.5 copy-start.15
  280.1 2.1 copy-start.24
  294.4 1.1 copy-start.19
  312.2 3.8 copy-start.12
  312.2 3.8 copy-start.14
  312.2 3.8 copy-start.25
  316.0 15.6 %copy-start.8 = (bf16[2304,2,96]{0,2,1:T(8,128)(2,1)}, bf16[2304,2,96]{0,2,1:T(8,128)(2,1)S(1)}, u32[]{:S(2)}) copy-start(bf16[2304,2,96]{0,2,1:T(8,128)(2,1)S(1)} %get-tuple-element.32) | copy-start | bytes 2654212
  316.7 0.9 copy-start.3
  331.6 2.8 copy-start.26
  331.6 3.2 copy-start.13
  334.4 3.3 copy-start.6
  334.4 1.8 copy-start.10
  336.2 1.5 copy-start.16
  337.7 1.2 copy-start.4
  337.7 1.7 copy-start.11
  340.9 1.6 copy-start.1
  379.0 35.1 %all-to-all-start.4 = ((bf16[1,384,2,6,192]{4,2,3,0,1:T(2,128)(2,1)}), bf16[1,384,2,6,192]{4,2,3,0,1:T(2,128)(2,1)}, u32[]{:S(2)}, u32[]{:S(2)}) async-start(bf16[1,384,2,6,192]{4,2,3,0,1:T(2,128)(2,1)} %copy.177), calls=%async_computation.4 | async-start | bytes 4718592 | tf_op jit(solution)/shard_map/all_to_all | solution.py:162
  416.1 0.9 copy-start.21
  416.2 1.0 copy-start.23
  438.9 541.7 %all-to-all-start.5 = ((bf16[1,24,768,192]{3,1,0,2:T(8,128)(2,1)}), bf16[1,24,768,192]{3,1,0,2:T(8,128)(2,1)}, u32[]{:S(2)}, u32[]{:S(2)}) async-start(bf16[1,24,768,192]{3,1,0,2:T(8,128)(2,1)} %copy.181), calls=%async_computation.5 | async-start | bytes 18874368 | tf_op jit(solution)/shard_map/all_to_all | solution.py:171
  446.2 531.2 %all-reduce.3.cloned.1.call-start = ((), (), s32[]{:S(2)}) async-start(), calls=%async_computation.6 | async-start | bytes 786432 | tf_op jit(solution)/shard_map/psum | solution.py:163
  446.2 1.7 copy-start.7
  446.2 1.7 copy-start.9
  448.0 1.2 copy-start.5
  449.1 1.5 copy-start.2
Sparse Core Ops, SparseCore 0:
  452.6 524.6 all-reduce.2
where the time goes:
time: 1030 us; the launch traced here: 1020 us
  waiting for transfers between devices  405 us (39%)
  local copies, waits for them, and re-layouts  254 us (25%)
  blocking collectives  231 us (22%)
  matrix products  57.5 us (6%)
  starting transfers between devices  40.6 us (4%)
  other arithmetic  18.4 us (2%)
  between operations  15.1 us (1%)
    psum x1, waiting for transfers between devices, on_device(): lax.psum((grad_one * scale, grad_two * scale, grad_bias * scale), ('dp',...  294 us
    psum x1, blocking collectives, on_device(): lax.psum((grad_one * scale, grad_two * scale, grad_bias * scale), ('dp',...  231 us
    all_to_all x1, waiting for transfers between devices, on_device(): lax.all_to_all(fields, 'lon', split_axis=3, concat_axis=2, tiled=True)  69.4 us
    unnamed x61, local copies, waits for them, and re-layouts  43.5 us
    all_to_all x1, waiting for transfers between devices, on_device(): lax.all_to_all(cotangent, 'lon', split_axis=3, concat_axis=2, tiled=True)  26.4 us
    all_to_all x2, local copies, waits for them, and re-layouts, on_device(): lax.all_to_all(fields, 'lon', split_axis=3, concat_axis=2, tiled=True)  26.4 us
    all_to_all x2, local copies, waits for them, and re-layouts, on_device(): lax.all_to_all(cotangent, 'lon', split_axis=3, concat_axis=2, tiled=True)  26.4 us
    convert_element_type x2, local copies, waits for them, and re-layouts, on_device(): grad_cells = (cot_cells.astype(jnp.float32) + spatial).astype(jnp.bfloat16)  24.7 us
  transfers between devices with their start and end apart: 7, of which 5 were waited for; matrix products, arithmetic and copies ran while one was open for 17% of the time, Pallas kernels for 0%

commit v1 on v0

v1 whole, which is shorter than its diff:
```python
import functools
import math

import jax
import jax.numpy as jnp
import numpy as np
from jax import lax
from jax.experimental import pallas as pl
from jax.experimental.pallas import tpu as pltpu
from jax.sharding import PartitionSpec as P

NLAT, NLON, KW, CH, BS, NBLK = 384, 768, 96, 384, 96, 4
HALF = NLON // 2
ROWS = 24
NG, GH = 3, 8
NJ = 3
ND = 8
NY = 4
SUB = 2 * GH
BLK = NG * SUB
QROWS = 4 * BLK
SPEC_ROWS = 4 * NLAT * KW

LON_NORM = 1.0 / math.sqrt(NLON)
LAT_NORM = 1.0 / math.sqrt(NLAT)
shrink_level = 0.05
gelu_coef = 0.044715
root = math.sqrt(2.0 / math.pi)

MESH = pl.DeviceIdType.MESH
F32, BF16 = jnp.float32, jnp.bfloat16


def cos_sin(phase_int, period):
    phase = phase_int.astype(np.float32) * np.float32(2.0 * math.pi / period)
    return np.cos(phase).astype(np.float32), np.sin(phase).astype(np.float32)


def tables():
    kk = np.arange(KW, dtype=np.int64)[:, None]
    ww = np.arange(NLON, dtype=np.int64)[None, :]
    cosine, sine = cos_sin(kk * ww % NLON, NLON)
    tw = np.stack([cosine, -sine], 1).reshape(2 * KW, 2, HALF).transpose(1, 0, 2)
    pp = np.arange(NLAT, dtype=np.int64)[:, None]
    hh = np.arange(NLAT, dtype=np.int64)[None, :]
    cosine, sine = cos_sin(pp * hh % NLAT, NLAT)
    th = np.stack([np.stack([cosine, sine], 0), np.stack([-sine, cosine], 0)], 0)
    th = th.transpose(0, 2, 1, 3).reshape(2 * NLAT, 2, NLAT // ROWS, NG, GH)
    th = th.transpose(0, 2, 3, 1, 4).reshape(2 * NLAT, 2 * NLAT)
    kind = jnp.bfloat16
    return (
        tw.astype(kind),
        np.ascontiguousarray(tw.transpose(0, 2, 1)).astype(kind),
        th.astype(kind),
        np.ascontiguousarray(th.T).astype(kind),
    )


def dot(a, b):
    return jnp.dot(a, b, preferred_element_type=F32)


def dot_nt(a, b):
    return lax.dot_general(a, b, (((1,), (1,)), ((), ())), preferred_element_type=F32)


def dot_tn(a, b):
    return lax.dot_general(a, b, (((0,), (0,)), ((), ())), preferred_element_type=F32)


def spectral_kernel(
    f_hbm,
    c_hbm,
    tw_ref,
    th_ref,
    tht_ref,
    wc1_ref,
    wc2_ref,
    bias_ref,
    back_hbm,
    g1_ref,
    g2_ref,
    gb_ref,
    fbuf,
    cbuf,
    ps,
    xs_f,
    xs_g,
    xr_f,
    xr_g,
    ys,
    yr,
    yb,
    yrb,
    zbuf,
    hbuf,
    dobuf,
    dzbuf,
    gmbuf,
    dsbuf,
    ld_sem,
    xl_sem,
    xsend,
    xrecv,
    yl_sem,
    ysend,
    yrecv,
):
    lat = lax.axis_index("lat")
    xhi = lax.axis_index("lon")
    dp = lax.axis_index("dp")
    y = lat // 4
    me = xhi * 4 + lax.rem(lat, 4)

    def device(yy, d):
        return (dp, yy * 4 + lax.rem(d, 4), d // 4)

    def load(which, g):
        src, dst = ((f_hbm, fbuf), (c_hbm, cbuf))[which]
        rows = pl.ds(g * GH, GH)
        return pltpu.make_async_copy(src.at[0, rows], dst.at[rows], ld_sem.at[which, g])

    for which in range(2):
        for g in range(NG):
            load(which, g).start()

    barrier = pltpu.get_barrier_semaphore()
    for i in range(1, ND):
        d = lax.rem(me + i, ND)
        pl.semaphore_signal(barrier, inc=1, device_id=device(y, d), device_id_type=MESH)
    for i in range(1, NY):
        yy = lax.rem(y + i, NY)
        pl.semaphore_signal(barrier, inc=1, device_id=device(yy, me), device_id_type=MESH)
    pl.semaphore_wait(barrier, ND - 1 + NY - 1)

    def x_refs(slot, d, frm):
        kind, i = slot // 3, slot % 3
        if kind == 0:
            return xs_f.at[i, d], xr_f.at[i, frm]
        if kind == 1:
            return xs_g.at[i, d], xr_g.at[i, frm]
        return yrb.at[i, :, pl.ds(pl.multiple_of(lax.rem(d, 4) * BLK, BLK), BLK)], back_hbm.at[i, frm]

    def x_copy(slot, d, frm):
        src, dst = x_refs(slot, d, frm)
        return pltpu.make_async_remote_copy(
            src_ref=src,
            dst_ref=dst,
            send_sem=xsend.at[slot, d],
            recv_sem=xrecv.at[slot, frm],
            device_id=device(y, d),
            device_id_type=MESH,
        )

    def x_local(slot):
        src, dst = x_refs(slot, me, me)
        return pltpu.make_async_copy(src, dst, xl_sem.at[slot])

    def x_start(slot):
        @pl.loop(1, ND)
        def _(i):
            x_copy(slot, lax.rem(me + i, ND), me).start()

        x_local(slot).start()

    def x_wait_recv(slot):
        @pl.loop(1, ND)
        def _(i):
            frm = lax.rem(me + ND - i, ND)
            x_copy(slot, frm, frm).wait_recv()

        x_local(slot).wait()

    def x_wait_send(slot):
        @pl.loop(1, ND)
        def _(i):
            x_copy(slot, lax.rem(me + i, ND), me).wait_send()

    def y_refs(slot, yy, frm):
        kind, j = slot // 3, slot % 3
        if kind < 2:
            return ys.at[kind, j, yy], yr.at[kind, j, frm]
        return yb.at[j, yy], yrb.at[j, frm]

    def y_copy(slot, yy, frm):
        src, dst = y_refs(slot, yy, frm)
        return pltpu.make_async_remote_copy(
            src_ref=src,
            dst_ref=dst,
            send_sem=ysend.at[slot, yy],
            recv_sem=yrecv.at[slot, frm],
            device_id=device(yy, me),
            device_id_type=MESH,
        )

    def y_local(slot):
        src, dst = y_refs(slot, y, y)
        return pltpu.make_async_copy(src, dst, yl_sem.at[slot])

    def y_start(slot):
        @pl.loop(1, NY)
        def _(i):
            y_copy(slot, lax.rem(y + i, NY), y).start()

        y_local(slot).start()

    def y_wait_recv(slot):
        @pl.loop(1, NY)
        def _(i):
            frm = lax.rem(y + NY - i, NY)
            y_copy(slot, frm, frm).wait_recv()

        y_local(slot).wait()

    def y_wait_send(slot):
        @pl.loop(1, NY)
        def _(i):
            y_copy(slot, lax.rem(y + i, NY), y).wait_send()

    def lon_group(which, g):
        buf = (fbuf, cbuf)[which]

        @pl.loop(0, GH)
        def _(h):
            part = dot(tw_ref[xhi], buf[g * GH + h])
            for ct in range(3):
                ps[ct, pl.ds(pl.multiple_of(h * 2 * KW, 2 * KW), 2 * KW), :] = part[
                    :, ct * 128 : (ct + 1) * 128
                ]

        @pl.loop(0, NJ * ND)
        def _(jd):
            j, d = jd // ND, lax.rem(jd, ND)
            for ky in range(NY):
                base = jd * (2 * NY) + 2 * ky
                for ct in range(3):
                    cols = pl.ds(ct * 128, 128)
                    tile = jnp.concatenate(
                        [ps[ct, pl.ds(base + r, GH, stride=2 * KW), :] for r in range(2)], 0
                    )
                    tile = (tile * LON_NORM).astype(BF16)
                    if which == 0:
                        xs_f[g, d, j * NY + ky, :, cols] = tile
                    else:
                        xs_g[j, d, ky, pl.ds(g * SUB, SUB), cols] = tile

    def x_sum_fields(j):
        @pl.loop(0, 4)
        def _(s):
            for ky in range(NY):
                for g in range(NG):
                    both = xr_f[g, s, j * NY + ky].astype(F32) + xr_f[g, s + 4, j * NY + ky].astype(
                        F32
                    )
                    rows = pl.ds(pl.multiple_of(s * BLK + g * SUB, SUB), SUB)
                    ys[0, j, ky, rows, :] = both.astype(BF16)

    def x_sum_cot(j):
        @pl.loop(0, 4)
        def _(s):
            for ky in range(NY):
                both = xr_g[j, s, ky].astype(F32) + xr_g[j, s + 4, ky].astype(F32)
                rows = pl.ds(pl.multiple_of(s * BLK, BLK), BLK)
                ys[1, j, ky, rows, :] = both.astype(BF16)

    TILE = 192

    def spectral(j):
        wave = (j * ND + me) * NY + y
        doubling = jnp.where(wave == 0, 1.0, 2.0).astype(F32) * LAT_NORM

        @pl.loop(0, 2)
        def _(t):
            rows = pl.ds(pl.multiple_of(t * TILE, TILE), TILE)
            for q in range(2):
                trows = pl.ds(pl.multiple_of(q * NLAT + t * TILE, TILE), TILE)
                cols = pl.ds(q * CH, CH)
                left = th_ref[trows, :]
                zbuf[rows, cols] = (
                    dot(left, yr[0, j].reshape(2 * NLAT, CH)) * LAT_NORM
                ).astype(BF16)
                gmbuf[rows, cols] = dot(left, yr[1, j].reshape(2 * NLAT, CH)) * doubling

        @pl.loop(0, 2)
        def _(t):
            rows = pl.ds(pl.multiple_of(t * TILE, TILE), TILE)
            o1 = dot(zbuf[rows, :], wc1_ref[...]) + bias_ref[...]
            square = o1 * o1
            tangent = jnp.tanh(root * (o1 + gelu_coef * o1 * square))
            hbuf[rows, :] = (0.5 * o1 * (1.0 + tangent)).astype(BF16)
            slope = 0.5 * (1.0 + tangent) + 0.5 * o1 * (1.0 - tangent * tangent) * root * (
                1.0 + 3.0 * gelu_coef * square
            )
            o2 = dot(hbuf[rows, :], wc2_ref[...])
            square = o2 * o2
            keep = square / (square + shrink_level * shrink_level)
            dobuf[rows, :] = (keep * gmbuf[rows, :]).astype(BF16)
            dh = dot_nt(dobuf[rows, :], wc2_ref[...])
            dz = (slope * dh).astype(BF16)
            dzbuf[rows, :] = dz
            gb_ref[...] += jnp.sum(dz.astype(F32), 0, keepdims=True)
            ds = dot_nt(dz, wc1_ref[...]).astype(BF16)
            for q in range(2):
                trows = pl.ds(pl.multiple_of(q * NLAT + t * TILE, TILE), TILE)
                dsbuf[trows, :] = ds[:, q * CH : (q + 1) * CH]

        @pl.loop(0, NY)
        def _(yy):
            rows = pl.ds(pl.multiple_of(yy * QROWS, QROWS), QROWS)
            yb[j, yy] = (dot(tht_ref[rows, :], dsbuf[...]) * LAT_NORM).astype(BF16)

        y_start(6 + j)

        re, im = pl.ds(0, CH), pl.ds(CH, CH)
        for zz, dd, out in ((zbuf, dzbuf, g1_ref), (hbuf, dobuf, g2_ref)):
            out[0] += dot_tn(zz[:, re], dd[:, re]) + dot_tn(zz[:, im], dd[:, im])
            out[1] += dot_tn(zz[:, re], dd[:, im]) - dot_tn(zz[:, im], dd[:, re])

    g1_ref[...] = jnp.zeros_like(g1_ref)
    g2_ref[...] = jnp.zeros_like(g2_ref)
    gb_ref[...] = jnp.zeros_like(gb_ref)

    for g in range(NG):
        load(0, g).wait()
        lon_group(0, g)
        x_start(g)
    for g in range(NG):
        load(1, g).wait()
        lon_group(1, g)
    x_wait_recv(0)
    x_wait_recv(1)
    x_start(3)
    x_wait_recv(2)
    x_start(4)
    for j in range(NJ):
        x_sum_fields(j)
        y_start(j)

    x_wait_recv(3)
    x_start(5)
    x_sum_cot(0)
    y_start(3)
    for j in range(NJ):
        y_wait_recv(j)
    y_wait_recv(3)
    spectral(0)
    x_wait_recv(4)
    x_sum_cot(1)
    y_start(4)
    y_wait_recv(6)
    x_start(6)
    y_wait_recv(4)
    spectral(1)
    x_wait_recv(5)
    x_sum_cot(2)
    y_start(5)
    y_wait_recv(7)
    x_start(7)
    y_wait_recv(5)
    spectral(2)
    y_wait_recv(8)
    x_start(8)
    for slot in range(9):
        if slot >= 6:
            x_wait_recv(slot)
        x_wait_send(slot)
        y_wait_send(slot)


def spectral_call(fields, cotangent, tw, th, tht, wc1, wc2, bias):
    vm = pl.BlockSpec(memory_space=pltpu.VMEM)
    hbm = pl.BlockSpec(memory_space=pl.ANY)
    dma = pltpu.SemaphoreType.DMA
    return pl.pallas_call(
        spectral_kernel,
        out_shape=(
            jax.ShapeDtypeStruct((NJ, ND, NY, BLK, CH), BF16),
            jax.ShapeDtypeStruct((2, CH, CH), F32),
            jax.ShapeDtypeStruct((2, CH, CH), F32),
            jax.ShapeDtypeStruct((1, 2 * CH), F32),
        ),
        in_specs=[hbm, hbm] + [vm] * 6,
        out_specs=(hbm, vm, vm, vm),
        scratch_shapes=[
            pltpu.VMEM((ROWS, HALF, CH), BF16),
            pltpu.VMEM((ROWS, HALF, CH), BF16),
            pltpu.VMEM((3, GH * 2 * KW, 128), F32),
            pltpu.VMEM((NG, ND, NJ * NY, SUB, CH), BF16),
            pltpu.VMEM((NJ, ND, NY, BLK, CH), BF16),
            pltpu.VMEM((NG, ND, NJ * NY, SUB, CH), BF16),
            pltpu.VMEM((NJ, ND, NY, BLK, CH), BF16),
            pltpu.VMEM((2, NJ, NY, QROWS, CH), BF16),
            pltpu.VMEM((2, NJ, NY, QROWS, CH), BF16),
            pltpu.VMEM((NJ, NY, QROWS, CH), BF16),
            pltpu.VMEM((NJ, NY, QROWS, CH), BF16),
            pltpu.VMEM((NLAT, 2 * CH), BF16),
            pltpu.VMEM((NLAT, 2 * CH), BF16),
            pltpu.VMEM((NLAT, 2 * CH), BF16),
            pltpu.VMEM((NLAT, 2 * CH), BF16),
            pltpu.VMEM((NLAT, 2 * CH), F32),
            pltpu.VMEM((2 * NLAT, CH), BF16),
            dma((2, NG)),
            dma((9,)),
            dma((9, ND)),
            dma((9, ND)),
            dma((9,)),
            dma((9, NY)),
            dma((9, NY)),
        ],
        compiler_params=pltpu.CompilerParams(
            collective_id=0, has_side_effects=True, vmem_limit_bytes=62 << 20
        ),
        cost_estimate=pl.CostEstimate(flops=10**10, bytes_accessed=3 * 10**7, transcendentals=10**6),
        name="spectral",
    )(fields, cotangent, tw, th, tht, wc1, wc2, bias)


def inverse_kernel(back_ref, cot_ref, twt_ref, out_ref, bs):
    xhi = lax.axis_index("lon")

    @pl.loop(0, NJ * ND)
    def _(jd):
        j, d = jd // ND, lax.rem(jd, ND)
        for ky in range(NY):
            rows = pl.ds(pl.multiple_of(jd * NY * SUB + ky * SUB, SUB), SUB)
            for ct in range(3):
                bs[ct, rows, :] = back_ref[j, d, ky, :, pl.ds(ct * 128, 128)].astype(F32)

    @pl.loop(0, GH)
    def _(h):
        spec = jnp.concatenate(
            [bs[ct, pl.ds(h, 2 * KW, stride=GH), :].astype(BF16) for ct in range(3)], 1
        )
        spatial = dot(twt_ref[xhi], spec) * LON_NORM
        out_ref[0, h] = (cot_ref[0, h].astype(F32) + spatial).astype(BF16)


def inverse_call(back, cotangent, twt):
    return pl.pallas_call(
        inverse_kernel,
        grid=(NG,),
        out_shape=jax.ShapeDtypeStruct((1, ROWS, HALF, CH), BF16),
        in_specs=[
            pl.BlockSpec((NJ, ND, NY, SUB, CH), lambda g: (0, 0, 0, g, 0)),
            pl.BlockSpec((1, GH, HALF, CH), lambda g: (0, g, 0, 0)),
            pl.BlockSpec((2, HALF, 2 * KW), lambda g: (0, 0, 0)),
        ],
        out_specs=pl.BlockSpec((1, GH, HALF, CH), lambda g: (0, g, 0, 0)),
        scratch_shapes=[pltpu.VMEM((3, GH * 2 * KW, 128), F32)],
        compiler_params=pltpu.CompilerParams(vmem_limit_bytes=48 << 20),
        cost_estimate=pl.CostEstimate(
            flops=1400 * 10**6, bytes_accessed=18 * 10**6, transcendentals=0
        ),
        name="inverse",
    )(back, cotangent, twt)


def dense_weight(weight):
    parts = [jax.scipy.linalg.block_diag(*[weight[n, r] for n in range(NBLK)]) for r in range(2)]
    return jnp.concatenate(
        [
            jnp.concatenate([parts[0], parts[1]], 1),
            jnp.concatenate([-parts[1], parts[0]], 1),
        ],
        0,
    )


def both_halves(mine):
    other = lax.ppermute(mine, "lon", [(0, 1), (1, 0)])
    first = lax.axis_index("lon") == 0
    return jnp.concatenate([jnp.where(first, mine, other), jnp.where(first, other, mine)], 0)


def on_device(fields, cotangent, w_first, w_second, bias_first):
    tw, twt, th, tht = tables()
    weights = both_halves(jnp.stack([w_first, w_second], 1))
    bias = both_halves(bias_first).transpose(1, 0, 2).reshape(1, 2 * CH)
    wc1, wc2 = dense_weight(weights[:, 0]), dense_weight(weights[:, 1])
    back, grad_one, grad_two, grad_bias = spectral_call(
        fields, cotangent, jnp.asarray(tw), jnp.asarray(th), jnp.asarray(tht), wc1, wc2, bias
    )
    grad_fields = inverse_call(back, cotangent, jnp.asarray(twt))

    def blocks(grad):
        return jnp.stack([grad[:, n * BS : (n + 1) * BS, n * BS : (n + 1) * BS] for n in range(NBLK)])

    grads = (blocks(grad_one), blocks(grad_two), grad_bias.reshape(2, NBLK, BS).transpose(1, 0, 2))
    grads = lax.psum(grads, ("dp", "lat", "lon"))
    scale = 1.0 / math.sqrt(SPEC_ROWS)
    here = lax.axis_index("lon") * 2
    grads = [lax.dynamic_slice_in_dim(grad * scale, here, 2, 0) for grad in grads]
    return (grad_fields, *grads)


def solution(mesh):
    placed = (
        P("dp", "lat", "lon", None),
        P("dp", "lat", "lon", None),
        P("lon", None, None, None),
        P("lon", None, None, None),
        P("lon", None, None),
    )
    return jax.shard_map(
        on_device,
        mesh=mesh,
        in_specs=placed,
        out_specs=(
            P("dp", "lat", "lon", None),
            P("lon", None, None, None),
            P("lon", None, None, None),
            P("lon", None, None),
        ),
        check_vma=False,
    )
```

time: 1030 us -> 355 us (0.34)
  waiting for transfers between devices: 405 us -> 70.3 us
  local copies, waits for them, and re-layouts: 254 us -> 5.52 us
  blocking collectives: 231 us -> 66.3 us
  Pallas kernels: 0 us -> 164 us
  matrix products: 57.5 us -> 0 us
  starting transfers between devices: 40.6 us -> 3.79 us
  other arithmetic: 18.4 us -> 30.3 us
    psum x1, waiting for transfers between devices: 294 us -> 64.7 us  [on_device(): grads = lax.psum(grads, ('dp', 'lat', 'lon'))]
    psum x1, blocking collectives: 231 us -> 66.3 us  [on_device(): grads = lax.psum(grads, ('dp', 'lat', 'lon'))]
    pallas_call x0 -> x2, Pallas kernels: none -> 164 us  [the longest x1 152 us: spectral_call(): pl.pallas_call(spectral_kernel, out_shape=(jax.ShapeDtypeStruct((NJ, ND,...]
    all_to_all x6 -> x0, waiting for transfers between devices: 112 us -> none  [the longest x1 69.4 us: on_device(): lax.all_to_all(fields, 'lon', split_axis=3, concat_axis=2, tiled=True)]
    all_to_all x12 -> x0, local copies, waits for them, and re-layouts: 81.8 us -> none  [the longest x2 26.4 us: on_device(): lax.all_to_all(fields, 'lon', split_axis=3, concat_axis=2, tiled=True)]
    dot_general x30 -> x0, matrix products: 57.5 us -> none  [the longest x8 14.8 us: matmul_fwd(): jnp.einsum('nbi,bio->nbo', left, right, preferred_element_type=jnp.float32)]
    unnamed x61 -> x6, local copies, waits for them, and re-layouts: 43.5 us -> 1.01 us
    all_to_all x6 -> x0, starting transfers between devices: 40.6 us -> none  [the longest x1 9.06 us: on_device(): lax.all_to_all(spec_a, 'lat', split_axis=3, concat_axis=1, tiled=True)]
  transfers between devices with their start and end apart: 7 -> 3, of which waited for: 5 -> 3; matrix products, arithmetic and copies ran while one was open for 17% -> 1% of each run, Pallas kernels for 0% -> 3%
where the time goes in v1:
time: 355 us
  Pallas kernels  164 us (46%)
  waiting for transfers between devices  70.3 us (20%)
  blocking collectives  66.3 us (19%)
  other arithmetic  30.3 us (9%)
  between operations  14.2 us (4%)
  local copies, waits for them, and re-layouts  5.52 us (2%)
  starting transfers between devices  3.79 us (1%)
    pallas_call x1, Pallas kernels, spectral_call(): pl.pallas_call(spectral_kernel, out_shape=(jax.ShapeDtypeStruct((NJ, ND,...  152 us
    psum x1, blocking collectives, on_device(): grads = lax.psum(grads, ('dp', 'lat', 'lon'))  66.3 us
    psum x1, waiting for transfers between devices, on_device(): grads = lax.psum(grads, ('dp', 'lat', 'lon'))  64.7 us
    concatenate x2, other arithmetic, dense_weight(): jnp.concatenate([jnp.concatenate([parts[0], parts[1]], 1), jnp.concatenat...  22 us
    pallas_call x1, Pallas kernels, inverse_call(): pl.pallas_call(inverse_kernel, grid=(NG,), out_shape=jax.ShapeDtypeStruct...  12.3 us
  transfers between devices with their start and end apart: 3, of which 3 were waited for; matrix products, arithmetic and copies ran while one was open for 1% of the time, Pallas kernels for 3%

profile of v1, /device:TPU:1, one launch (start us, length us, event | category | flops | bytes accessed | tf_op | source)
XLA Modules:
  0.0 354.9 jit_solution(9380865119387037692)
XLA Ops:
  7.2 0.0 all-reduce.19.cloned.1.call-start
  7.2 3.7 %collective-permute-start.1 = (f32[2,2,96]{2,1,0:T(2,128)}, f32[2,2,96]{2,1,0:T(2,128)S(1)}, u32[]{:S(2)}, u32[]{:S(2)}) collective-permute-start(f32[2,2,96]{2,1,0:T(2,128)} %param.13), channel_id=1, source_target_pairs={{0,1},{1,0},{2,3},{3,2},{4,5},{5,4},{6,7},{7,6},{8,9},{9,8},{10,11... | collective-permute-start | bytes 4616 | tf_op jit(solution)/shard_map/ppermute | solution.py:470
  10.9 1.0 pad_maximum_fusion.3
  11.8 0.1 collective-permute-start
  11.9 0.1 collective-permute-done.1
  12.1 0.7 broadcast_select_fusion.3
  12.8 0.7 reshape.14.bias_ref
  13.4 5.5 %collective-permute-done = bf16[2,2,2,96,96]{4,3,2,0,1:T(8,128)(2,1)S(1)} collective-permute-done((bf16[2,2,2,96,96]{4,3,2,0,1:T(8,128)(2,1)S(1)}, bf16[2,2,2,96,96]{4,3,2,0,1:T(8,128)(2,1)S(1)}, u32[]{:S(2)}, u32[]{:S(2)}) %collective-permute-start) | collective-permute-done | bytes 147488 | tf_op jit(solution)/shard_map/ppermute | solution.py:470
  18.9 1.0 broadcast_select_fusion
  19.9 0.1 fusion.2
  20.0 0.1 pad.67
  20.1 0.1 pad.66
  20.2 0.1 pad.65
  20.3 0.1 pad.57
  20.4 0.1 pad.58
  20.5 0.1 pad.59
  20.6 0.1 pad.63
  20.6 0.1 pad.62
  20.7 0.1 pad.61
  20.9 0.1 pad.53
  21.0 0.1 pad.54
  21.0 0.1 pad.55
  21.1 0.1 maximum_negate_fusion
  21.2 0.1 maximum_negate_fusion.1
  21.2 11.1 %maximum_maximum_fusion.wc1_ref = bf16[768,768]{1,0:T(8,128)(2,1)} fusion(bf16[96,384]{1,0:T(8,128)(2,1)S(1)} %pad.55, bf16[96,384]{1,0:T(8,128)(2,1)S(1)} %pad.54, bf16[96,384]{1,0:T(8,128)(2,1)S(1)} %pad.53, bf16[96,384]{1,0:T(8,128)(2,1)S(1)} %pad.52, bf16[384,384]{1,0:T(8,128)(2,1)S(1)} %maximum_negate_fusion, bf16[96,384]{1,0:T(8,128)(2,1)S(1)} %pad.59, ...), kind=kLoop, calls=%fused_computation | loop fusion | flops 15335424 | bytes 2064384 | tf_op jit(solution)/shard_map/concatenate | solution.py:460
  32.3 10.9 %maximum_maximum_fusion.1.wc2_ref = bf16[768,768]{1,0:T(8,128)(2,1)} fusion(bf16[96,384]{1,0:T(8,128)(2,1)S(1)} %pad.63, bf16[96,384]{1,0:T(8,128)(2,1)S(1)} %pad.62, bf16[96,384]{1,0:T(8,128)(2,1)S(1)} %pad.61, bf16[96,384]{1,0:T(8,128)(2,1)S(1)} %pad.60, bf16[384,384]{1,0:T(8,128)(2,1)S(1)} %maximum_negate_fusion.1, bf16[96,384]{1,0:T(8,128)(2,1)S(1)} %pad.67, ...), kind=kLoop, calls=%fused_computation.1 | loop fusion | flops 15335424 | bytes 2064384 | tf_op jit(solution)/shard_map/concatenate | solution.py:460
  43.2 152.2 %spectral.1 = (bf16[3,8,4,48,384]{4,3,2,1,0:T(8,128)(2,1)}, f32[2,384,384]{2,1,0:T(8,128)}, f32[2,384,384]{2,1,0:T(8,128)}, f32[1,768]{1,0:T(1,128)}) custom-call(bf16[1,24,384,384]{3,2,1,0:T(8,128)(2,1)} %f_hbm.1, bf16[1,24,384,384]{3,2,1,0:T(8,128)(2,1)} %cot_ref.1, bf16[2,192,384]{2,1,0:T(8,128)(2,1)} %constant.27.clone.tw_ref, ...), custom_call_target="tpu_custom_call" | custom-call | flops 10000000000 | bytes 30000000 | tf_op jit(solution)/shard_map/spectral/pallas_call | solution.py:374
  195.5 0.0 copy-start.2
  195.5 0.0 copy-start
  195.5 1.4 slice_bitcast_fusion.7
  196.9 1.3 slice_bitcast_fusion.3
  198.2 0.8 pad_maximum_fusion
  199.0 0.8 pad_maximum_fusion.1
  199.8 0.0 all-reduce.19.cloned.1.call-update
  199.8 0.0 copy-done.2
  199.9 0.1 reshape.15
  200.0 66.3 %psum.23 = f32[4,2,96]{2,1,0:T(2,128)S(1)} all-reduce(f32[4,2,96]{2,1,0:T(2,128)S(1)} %bitcast.63), channel_id=1, replica_groups=mesh['dp'=4,'lat'=16,'lon'=2] {'dp','lat','lon'}, use_global_device_ids=true, to_apply=%region_2.3 | all-reduce | flops 768 | bytes 6144 | tf_op jit(solution)/shard_map/psum | solution.py:489
  266.3 0.6 dynamic-slice_multiply_fusion.2
  266.9 0.0 copy-done
  266.9 0.0 copy-start.1
  266.9 1.0 copy-done.1
  267.9 12.3 %inverse.1 = bf16[1,24,384,384]{3,2,1,0:T(8,128)(2,1)} custom-call(bf16[3,8,4,48,384]{4,3,2,1,0:T(8,128)(2,1)S(1)} %copy-done, bf16[1,24,384,384]{3,2,1,0:T(8,128)(2,1)} %cot_ref.1, bf16[2,384,192]{2,1,0:T(8,128)(2,1)S(1)} %copy-done.1), custom_call_target="tpu_custom_call" | custom-call | flops 1400000000 | bytes 18000000 | tf_op jit(solution)/shard_map/inverse/pallas_call | solution.py:439
  280.1 64.7 %all-reduce.19.cloned.1.call-done = (f32[4,2,96,96]{3,2,1,0:T(8,128)}, f32[4,2,96,96]{3,2,1,0:T(8,128)}) async-done(((f32[4,2,96,96]{3,2,1,0:T(8,128)}, f32[4,2,96,96]{3,2,1,0:T(8,128)}), (f32[4,2,96,96]{3,2,1,0:T(8,128)}, f32[4,2,96,96]{3,2,1,0:T(8,128)})) %all-reduce.19.cloned.1.call-update) | async-done | bytes 589840 | tf_op jit(solution)/shard_map/psum | solution.py:489
  344.8 1.6 dynamic-slice_multiply_fusion.1
  346.4 1.6 dynamic-slice_multiply_fusion
  (9 shorter events, 0.1 us)
Async XLA Ops:
  7.2 337.6 %all-reduce.19.cloned.1.call-start = ((), (), s32[]{:S(2)}) async-start(), calls=%async_computation | async-start | bytes 1572864 | tf_op jit(solution)/shard_map/psum | solution.py:489
  7.2 4.8 %collective-permute-start.1 = (f32[2,2,96]{2,1,0:T(2,128)}, f32[2,2,96]{2,1,0:T(2,128)S(1)}, u32[]{:S(2)}, u32[]{:S(2)}) collective-permute-start(f32[2,2,96]{2,1,0:T(2,128)} %param.13), channel_id=1, source_target_pairs={{0,1},{1,0},{2,3},{3,2},{4,5},{5,4},{6,7},{7,6},{8,9},{9,8},{10,11... | collective-permute-start | bytes 4616 | tf_op jit(solution)/shard_map/ppermute | solution.py:470
  11.8 7.0 %collective-permute-start = (bf16[2,2,2,96,96]{4,3,2,0,1:T(8,128)(2,1)S(1)}, bf16[2,2,2,96,96]{4,3,2,0,1:T(8,128)(2,1)S(1)}, u32[]{:S(2)}, u32[]{:S(2)}) collective-permute-start(bf16[2,2,2,96,96]{4,3,2,0,1:T(8,128)(2,1)S(1)} %pad_maximum_fusion.3), channel_id=1, source_target_pairs={{0,1},{1,0},{2,3},{3,2},{4,5},{5,4},{6,7},{7,6},{8,9},{9,8},{10,11... | collective-permute-start | bytes 442376 | tf_op jit(solution)/shard_map/ppermute | solution.py:470
  195.5 4.4 %copy-start.2 = (f32[1,768]{1,0:T(1,128)S(1)}, f32[1,768]{1,0:T(1,128)}, u32[]{:S(2)}) copy-start(f32[1,768]{1,0:T(1,128)} %get-tuple-element.11) | copy-start | bytes 9220
  195.5 71.4 %copy-start = (bf16[3,8,4,48,384]{4,3,2,1,0:T(8,128)(2,1)S(1)}, bf16[3,8,4,48,384]{4,3,2,1,0:T(8,128)(2,1)}, u32[]{:S(2)}) copy-start(bf16[3,8,4,48,384]{4,3,2,1,0:T(8,128)(2,1)} %get-tuple-element.8.back_ref) | copy-start | bytes 10616836
  266.9 1.0 copy-start.1
Sparse Core Ops, SparseCore 0:
  200.0 144.8 all-reduce.18

commit v2 on v1

--- a/solution.py
+++ b/solution.py
@@ -16,6 +16,7 @@
 NJ = 3
 ND = 8
 NY = 4
+NZ = 4
 SUB = 2 * GH
 BLK = NG * SUB
 QROWS = 4 * BLK
@@ -74,13 +75,27 @@
     tw_ref,
     th_ref,
     tht_ref,
+    w1_ref,
+    w2_ref,
+    b1_ref,
+    back_hbm,
+    gout_ref,
+    gbout_ref,
+    w_all,
+    b_all,
     wc1_ref,
     wc2_ref,
     bias_ref,
-    back_hbm,
-    g1_ref,
-    g2_ref,
+    gacc,
     gb_ref,
+    gz,
+    gzr,
+    gy,
+    gyr,
+    gd,
+    gdr,
+    gyo,
+    gzo,
     fbuf,
     cbuf,
     ps,
@@ -105,6 +120,11 @@
     yl_sem,
     ysend,
     yrecv,
+    wl_sem,
+    wsend,
+    wrecv,
+    gsend,
+    grecv,
 ):
     lat = lax.axis_index("lat")
     xhi = lax.axis_index("lon")
@@ -112,8 +132,8 @@
     y = lat // 4
     me = xhi * 4 + lax.rem(lat, 4)
 
-    def device(yy, d):
-        return (dp, yy * 4 + lax.rem(d, 4), d // 4)
+    def device(yy, d, zz=dp):
+        return (zz, yy * 4 + lax.rem(d, 4), d // 4)
 
     def load(which, g):
         src, dst = ((f_hbm, fbuf), (c_hbm, cbuf))[which]
@@ -131,7 +151,61 @@
     for i in range(1, NY):
         yy = lax.rem(y + i, NY)
         pl.semaphore_signal(barrier, inc=1, device_id=device(yy, me), device_id_type=MESH)
-    pl.semaphore_wait(barrier, ND - 1 + NY - 1)
+    for i in range(1, NZ):
+        zz = lax.rem(dp + i, NZ)
+        pl.semaphore_signal(barrier, inc=1, device_id=device(y, me, zz), device_id_type=MESH)
+    pl.semaphore_wait(barrier, ND - 1 + NY - 1 + NZ - 1)
+
+    def weight_refs(i):
+        return ((w1_ref, w_all.at[0, xhi]), (w2_ref, w_all.at[1, xhi]), (b1_ref, b_all.at[xhi]))[i]
+
+    def weight_copy(i):
+        src, dst = weight_refs(i)
+        return pltpu.make_async_remote_copy(
+            src_ref=src,
+            dst_ref=dst,
+            send_sem=wsend.at[i],
+            recv_sem=wrecv.at[i],
+            device_id=device(y, lax.rem(me + 4, ND)),
+            device_id_type=MESH,
+        )
+
+    def weight_local(i):
+        src, dst = weight_refs(i)
+        return pltpu.make_async_copy(src, dst, wl_sem.at[i])
+
+    def weights_start():
+        for i in range(3):
+            weight_copy(i).start()
+            weight_local(i).start()
+
+    def weights_build():
+        for i in range(3):
+            weight_copy(i).wait()
+            weight_local(i).wait()
+        row = lax.broadcasted_iota(jnp.int32, (BS, CH), 0)
+        col = lax.broadcasted_iota(jnp.int32, (BS, CH), 1)
+        bias = jnp.zeros((2, CH), F32)
+        for n in range(NBLK):
+            spread = col == row + n * BS
+            bias += jnp.dot(
+                b_all[n // 2, n % 2],
+                spread.astype(F32),
+                precision=lax.Precision.HIGHEST,
+                preferred_element_type=F32,
+            )
+            spread = spread.astype(F32).astype(BF16)
+            top, low = pl.ds(n * BS, BS), pl.ds(CH + n * BS, BS)
+            re, im = pl.ds(0, CH), pl.ds(CH, CH)
+            for i, out in enumerate((wc1_ref, wc2_ref)):
+                real = dot(w_all[i, n // 2, n % 2, 0], spread)
+                imag = dot(w_all[i, n // 2, n % 2, 1], spread)
+                out[top, re] = real.astype(BF16)
+                out[low, im] = real.astype(BF16)
+                out[top, im] = imag.astype(BF16)
+                out[low, re] = (-imag).astype(BF16)
+        for r in range(2):
+            bias_ref[:, pl.ds(r * CH, CH)] = bias[r : r + 1]
 
     def x_refs(slot, d, frm):
         kind, i = slot // 3, slot % 3
@@ -312,12 +386,92 @@
         y_start(6 + j)
 
         re, im = pl.ds(0, CH), pl.ds(CH, CH)
-        for zz, dd, out in ((zbuf, dzbuf, g1_ref), (hbuf, dobuf, g2_ref)):
-            out[0] += dot_tn(zz[:, re], dd[:, re]) + dot_tn(zz[:, im], dd[:, im])
-            out[1] += dot_tn(zz[:, re], dd[:, im]) - dot_tn(zz[:, im], dd[:, re])
-
-    g1_ref[...] = jnp.zeros_like(g1_ref)
-    g2_ref[...] = jnp.zeros_like(g2_ref)
+        for i, (zz, dd) in enumerate(((zbuf, dzbuf), (hbuf, dobuf))):
+            gacc[2 * i] += dot_tn(zz[:, re], dd[:, re]) + dot_tn(zz[:, im], dd[:, im])
+            gacc[2 * i + 1] += dot_tn(zz[:, re], dd[:, im]) - dot_tn(zz[:, im], dd[:, re])
+
+    def grad_copy(stage, to, frm):
+        src, dst, target = (
+            lambda: (gz.at[to], gzr.at[frm], device(y, me, to)),
+            lambda: (gy.at[to], gyr.at[frm], device(to, me)),
+            lambda: (gd, gdr.at[frm], device(y, to)),
+            lambda: (gd.at[pl.ds(0, BS // NY)], gyo.at[frm], device(to, me)),
+            lambda: (gyo, gzo.at[frm], device(y, me, to)),
+        )[stage]()
+        return pltpu.make_async_remote_copy(
+            src_ref=src,
+            dst_ref=dst,
+            send_sem=gsend.at[stage, to],
+            recv_sem=grecv.at[stage, frm],
+            device_id=target,
+            device_id_type=MESH,
+        )
+
+    stage_size = (NZ, NY, ND, NY, NZ)
+    stage_place = (dp, y, me, y, dp)
+
+    def grad_start(stage):
+        here, size = stage_place[stage], stage_size[stage]
+
+        @pl.loop(1, size)
+        def _(i):
+            grad_copy(stage, lax.rem(here + i, size), here).start()
+
+    def grad_wait(stage):
+        here, size = stage_place[stage], stage_size[stage]
+
+        @pl.loop(1, size)
+        def _(i):
+            frm = lax.rem(here + size - i, size)
+            grad_copy(stage, frm, frm).wait_recv()
+
+        @pl.loop(1, size)
+        def _(i):
+            grad_copy(stage, lax.rem(here + i, size), here).wait_send()
+
+    def grad_begin():
+        lane = lax.broadcasted_iota(jnp.int32, (BS, CH), 1)
+        line = lax.broadcasted_iota(jnp.int32, (8, CH), 0)
+        both = [jnp.broadcast_to(gb_ref[:, pl.ds(r * CH, CH)], (8, CH)) for r in range(2)]
+        sums = jnp.where(line == 0, both[0], jnp.where(line == 1, both[1], 0.0))
+        for i in range(NZ):
+            part = gacc[i, pl.ds(0, BS), :]
+            for n in range(1, NBLK):
+                part = jnp.where(lane >= n * BS, gacc[i, pl.ds(n * BS, BS), :], part)
+            gz[i, pl.ds(0, BS), :] = part
+            gz[i, pl.ds(BS, 8), :] = sums
+        gzr[dp] = gz[dp]
+        grad_start(0)
+
+    def grad_finish():
+        part = BS // NY
+        grad_wait(0)
+        total = gzr[0] + gzr[1] + gzr[2] + gzr[3]
+        for i in range(NY):
+            gy[i, pl.ds(0, part), :] = total[i * part : (i + 1) * part]
+            gy[i, pl.ds(part, 8), :] = total[BS:]
+        gyr[y] = gy[y]
+        grad_start(1)
+        grad_wait(1)
+        gd[...] = gyr[0] + gyr[1] + gyr[2] + gyr[3]
+        gdr[me] = gd[...]
+        grad_start(2)
+        grad_wait(2)
+        total = gdr[0]
+        for i in range(1, ND):
+            total += gdr[i]
+        gd[...] = total
+        gbout_ref[...] = total[part:]
+        gyo[y] = total[:part]
+        grad_start(3)
+        grad_wait(3)
+        gzo[dp] = gyo[...]
+        grad_start(4)
+        grad_wait(4)
+        gout_ref[...] = gzo[...]
+
+    weights_start()
+    gacc[...] = jnp.zeros_like(gacc)
     gb_ref[...] = jnp.zeros_like(gb_ref)
 
     for g in range(NG):
@@ -327,6 +481,7 @@
     for g in range(NG):
         load(1, g).wait()
         lon_group(1, g)
+    weights_build()
     x_wait_recv(0)
     x_wait_recv(1)
     x_start(3)
@@ -358,8 +513,10 @@
     x_start(7)
     y_wait_recv(5)
     spectral(2)
+    grad_begin()
     y_wait_recv(8)
     x_start(8)
+    grad_finish()
     for slot in range(9):
         if slot >= 6:
             x_wait_recv(slot)
@@ -367,7 +524,7 @@
         y_wait_send(slot)
 
 
-def spectral_call(fields, cotangent, tw, th, tht, wc1, wc2, bias):
+def spectral_call(fields, cotangent, tw, th, tht, w_first, w_second, bias):
     vm = pl.BlockSpec(memory_space=pltpu.VMEM)
     hbm = pl.BlockSpec(memory_space=pl.ANY)
     dma = pltpu.SemaphoreType.DMA
@@ -375,13 +532,27 @@
         spectral_kernel,
         out_shape=(
             jax.ShapeDtypeStruct((NJ, ND, NY, BLK, CH), BF16),
-            jax.ShapeDtypeStruct((2, CH, CH), F32),
-            jax.ShapeDtypeStruct((2, CH, CH), F32),
-            jax.ShapeDtypeStruct((1, 2 * CH), F32),
+            jax.ShapeDtypeStruct((NZ, NY, BS // NY, CH), F32),
+            jax.ShapeDtypeStruct((8, CH), F32),
         ),
         in_specs=[hbm, hbm] + [vm] * 6,
-        out_specs=(hbm, vm, vm, vm),
+        out_specs=(hbm, vm, vm),
         scratch_shapes=[
+            pltpu.VMEM((2, 2, 2, 2, BS, BS), BF16),
+            pltpu.VMEM((2, 2, 2, BS), F32),
+            pltpu.VMEM((2 * CH, 2 * CH), BF16),
+            pltpu.VMEM((2 * CH, 2 * CH), BF16),
+            pltpu.VMEM((1, 2 * CH), F32),
+            pltpu.VMEM((4, CH, CH), F32),
+            pltpu.VMEM((1, 2 * CH), F32),
+            pltpu.VMEM((NZ, BS + 8, CH), F32),
+            pltpu.VMEM((NZ, BS + 8, CH), F32),
+            pltpu.VMEM((NY, BS // NY + 8, CH), F32),
+            pltpu.VMEM((NY, BS // NY + 8, CH), F32),
+            pltpu.VMEM((BS // NY + 8, CH), F32),
+            pltpu.VMEM((ND, BS // NY + 8, CH), F32),
+            pltpu.VMEM((NY, BS // NY, CH), F32),
+            pltpu.VMEM((NZ, NY, BS // NY, CH), F32),
             pltpu.VMEM((ROWS, HALF, CH), BF16),
             pltpu.VMEM((ROWS, HALF, CH), BF16),
             pltpu.VMEM((3, GH * 2 * KW, 128), F32),
@@ -406,16 +577,21 @@
             dma((9,)),
             dma((9, NY)),
             dma((9, NY)),
+            dma((3,)),
+            dma((3,)),
+            dma((3,)),
+            dma((5, ND)),
+            dma((5, ND)),
         ],
         compiler_params=pltpu.CompilerParams(
             collective_id=0, has_side_effects=True, vmem_limit_bytes=62 << 20
         ),
         cost_estimate=pl.CostEstimate(flops=10**10, bytes_accessed=3 * 10**7, transcendentals=10**6),
         name="spectral",
-    )(fields, cotangent, tw, th, tht, wc1, wc2, bias)
-
-
-def inverse_kernel(back_ref, cot_ref, twt_ref, out_ref, bs):
+    )(fields, cotangent, tw, th, tht, w_first, w_second, bias)
+
+
+def inverse_kernel(back_ref, cot_ref, twt_ref, grad_ref, bias_ref, out_ref, g1_ref, g2_ref, gb_ref, bs):
     xhi = lax.axis_index("lon")
 
     @pl.loop(0, NJ * ND)
@@ -434,63 +610,66 @@
         spatial = dot(twt_ref[xhi], spec) * LON_NORM
         out_ref[0, h] = (cot_ref[0, h].astype(F32) + spatial).astype(BF16)
 
-
-def inverse_call(back, cotangent, twt):
+    @pl.when(pl.program_id(0) == 0)
+    def _():
+        scale = 1.0 / math.sqrt(SPEC_ROWS)
+        row = lax.broadcasted_iota(jnp.int32, (CH, BS), 0)
+        col = lax.broadcasted_iota(jnp.int32, (CH, BS), 1)
+        for m in range(2):
+            pick = (row == col + (2 * xhi + m) * BS).astype(F32)
+
+            def take(value):
+                return scale * jnp.dot(
+                    value, pick, precision=lax.Precision.HIGHEST, preferred_element_type=F32
+                )
+
+            for r in range(2):
+                g1_ref[m, r] = take(grad_ref[r].reshape(BS, CH))
+                g2_ref[m, r] = take(grad_ref[2 + r].reshape(BS, CH))
+            gb_ref[m] = take(bias_ref[...])[:2]
+
+
+def inverse_call(back, cotangent, twt, grads, bias):
+    def whole(*shape):
+        return pl.BlockSpec(shape, lambda g: (0,) * len(shape))
+
     return pl.pallas_call(
         inverse_kernel,
         grid=(NG,),
-        out_shape=jax.ShapeDtypeStruct((1, ROWS, HALF, CH), BF16),
+        out_shape=(
+            jax.ShapeDtypeStruct((1, ROWS, HALF, CH), BF16),
+            jax.ShapeDtypeStruct((2, 2, BS, BS), F32),
+            jax.ShapeDtypeStruct((2, 2, BS, BS), F32),
+            jax.ShapeDtypeStruct((2, 2, BS), F32),
+        ),
         in_specs=[
             pl.BlockSpec((NJ, ND, NY, SUB, CH), lambda g: (0, 0, 0, g, 0)),
             pl.BlockSpec((1, GH, HALF, CH), lambda g: (0, g, 0, 0)),
-            pl.BlockSpec((2, HALF, 2 * KW), lambda g: (0, 0, 0)),
+            whole(2, HALF, 2 * KW),
+            whole(NZ, NY, BS // NY, CH),
+            whole(8, CH),
         ],
-        out_specs=pl.BlockSpec((1, GH, HALF, CH), lambda g: (0, g, 0, 0)),
+        out_specs=(
+            pl.BlockSpec((1, GH, HALF, CH), lambda g: (0, g, 0, 0)),
+            whole(2, 2, BS, BS),
+            whole(2, 2, BS, BS),
+            whole(2, 2, BS),
+        ),
         scratch_shapes=[pltpu.VMEM((3, GH * 2 * KW, 128), F32)],
         compiler_params=pltpu.CompilerParams(vmem_limit_bytes=48 << 20),
         cost_estimate=pl.CostEstimate(
             flops=1400 * 10**6, bytes_accessed=18 * 10**6, transcendentals=0
         ),
         name="inverse",
-    )(back, cotangent, twt)
-
-
-def dense_weight(weight):
-    parts = [jax.scipy.linalg.block_diag(*[weight[n, r] for n in range(NBLK)]) for r in range(2)]
-    return jnp.concatenate(
-        [
-            jnp.concatenate([parts[0], parts[1]], 1),
-            jnp.concatenate([-parts[1], parts[0]], 1),
-        ],
-        0,
+    )(back, cotangent, twt, grads, bias)
+
+
+def on_device(fields, cotangent, w_first, w_second, bias_first):
+    tw, twt, th, tht = (jnp.asarray(table) for table in tables())
+    back, grads, bias = spectral_call(
+        fields, cotangent, tw, th, tht, w_first, w_second, bias_first
     )
-
-
-def both_halves(mine):
-    other = lax.ppermute(mine, "lon", [(0, 1), (1, 0)])
-    first = lax.axis_index("lon") == 0
-    return jnp.concatenate([jnp.where(first, mine, other), jnp.where(first, other, mine)], 0)
-
-
-def on_device(fields, cotangent, w_first, w_second, bias_first):
-    tw, twt, th, tht = tables()
-    weights = both_halves(jnp.stack([w_first, w_second], 1))
-    bias = both_halves(bias_first).transpose(1, 0, 2).reshape(1, 2 * CH)
-    wc1, wc2 = dense_weight(weights[:, 0]), dense_weight(weights[:, 1])
-    back, grad_one, grad_two, grad_bias = spectral_call(
-        fields, cotangent, jnp.asarray(tw), jnp.asarray(th), jnp.asarray(tht), wc1, wc2, bias
-    )
-    grad_fields = inverse_call(back, cotangent, jnp.asarray(twt))
-
-    def blocks(grad):
-        return jnp.stack([grad[:, n * BS : (n + 1) * BS, n * BS : (n + 1) * BS] for n in range(NBLK)])
-
-    grads = (blocks(grad_one), blocks(grad_two), grad_bias.reshape(2, NBLK, BS).transpose(1, 0, 2))
-    grads = lax.psum(grads, ("dp", "lat", "lon"))
-    scale = 1.0 / math.sqrt(SPEC_ROWS)
-    here = lax.axis_index("lon") * 2
-    grads = [lax.dynamic_slice_in_dim(grad * scale, here, 2, 0) for grad in grads]
-    return (grad_fields, *grads)
+    return inverse_call(back, cotangent, twt, grads, bias)
 
 
 def solution(mesh):

time: 355 us -> 191 us (0.54)
  waiting for transfers between devices: 70.3 us -> 0 us
  blocking collectives: 66.3 us -> 0 us
  other arithmetic: 30.3 us -> 0 us
  Pallas kernels: 164 us -> 186 us
  between operations: 14.2 us -> 0.67 us
  starting transfers between devices: 3.79 us -> 0 us
    psum x1 -> x0, blocking collectives: 66.3 us -> none  [on_device(): grads = lax.psum(grads, ('dp', 'lat', 'lon'))]
    psum x1 -> x0, waiting for transfers between devices: 64.7 us -> none  [on_device(): grads = lax.psum(grads, ('dp', 'lat', 'lon'))]
    concatenate x2 -> x0, other arithmetic: 22 us -> none  [dense_weight(): jnp.concatenate([jnp.concatenate([parts[0], parts[1]], 1), jnp.concatenat...]
    pallas_call x1, Pallas kernels: 152 us -> 172 us  [spectral_call(): pl.pallas_call(spectral_kernel, out_shape=(jax.ShapeDtypeStruct((NJ, ND,...]
    ppermute x2 -> x0, waiting for transfers between devices: 5.57 us -> none  [both_halves(): other = lax.ppermute(mine, 'lon', [(0, 1), (1, 0)])]
    mul x3 -> x0, other arithmetic: 3.82 us -> none  [on_device(): grad * scale]
    ppermute x2 -> x0, starting transfers between devices: 3.75 us -> none  [both_halves(): other = lax.ppermute(mine, 'lon', [(0, 1), (1, 0)])]
  transfers between devices with their start and end apart: 3 -> 0, of which waited for: 3 -> 0; matrix products, arithmetic and copies ran while one was open for 1% -> 0% of each run, Pallas kernels for 3% -> 0%
where the time goes in v2:
time: 191 us; the launch traced here: 190 us
  Pallas kernels  186 us (97%)
  local copies, waits for them, and re-layouts  3.77 us (2%)
    pallas_call x1, Pallas kernels, spectral_call(): pl.pallas_call(spectral_kernel, out_shape=(jax.ShapeDtypeStruct((NJ, ND,...  172 us
    pallas_call x1, Pallas kernels, inverse_call(): pl.pallas_call(inverse_kernel, grid=(NG,), out_shape=(jax.ShapeDtypeStruc...  13.8 us

profile of v2, /device:TPU:1, one launch (start us, length us, event | category | flops | bytes accessed | tf_op | source)
XLA Modules:
  0.0 190.2 jit_solution(17366005619670355137)
XLA Ops:
  0.6 0.0 copy-start.2
  0.6 171.9 %spectral.1 = (bf16[3,8,4,48,384]{4,3,2,1,0:T(8,128)(2,1)}, f32[4,4,24,384]{3,2,1,0:T(8,128)}, f32[8,384]{1,0:T(8,128)}) custom-call(bf16[1,24,384,384]{3,2,1,0:T(8,128)(2,1)} %f_hbm.1, bf16[1,24,384,384]{3,2,1,0:T(8,128)(2,1)} %cot_ref.1, bf16[2,192,384]{2,1,0:T(8,128)(2,1)} %constant.8.clone.tw_ref, bf16[768,768]{1,0:T(8,128)(2,1)} %constant.10.clone.th_ref, ...), custom_call_target="tpu_custom_call" | custom-call | flops 10000000000 | bytes 30000000 | tf_op jit(solution)/shard_map/spectral/pallas_call | solution.py:531
  172.6 0.0 copy-done.2
  172.6 0.0 copy-start
  172.6 2.0 %copy-done = bf16[3,8,4,48,384]{4,3,2,1,0:T(8,128)(2,1)S(1)} copy-done((bf16[3,8,4,48,384]{4,3,2,1,0:T(8,128)(2,1)S(1)}, bf16[3,8,4,48,384]{4,3,2,1,0:T(8,128)(2,1)}, u32[]{:S(2)}) %copy-start) | copy-done | bytes 3538968
  174.6 0.0 copy-start.1
  174.6 1.1 copy-done.1
  175.7 0.0 copy-start.3
  175.7 0.7 copy-done.3
  176.4 13.8 %inverse.1 = (bf16[1,24,384,384]{3,2,1,0:T(8,128)(2,1)}, f32[2,2,96,96]{3,2,1,0:T(8,128)}, f32[2,2,96,96]{3,2,1,0:T(8,128)}, f32[2,2,96]{2,1,0:T(2,128)}) custom-call(bf16[3,8,4,48,384]{4,3,2,1,0:T(8,128)(2,1)S(1)} %copy-done, bf16[1,24,384,384]{3,2,1,0:T(8,128)(2,1)} %cot_ref.1, bf16[2,384,192]{2,1,0:T(8,128)(2,1)S(1)} %copy-done.2, ...), custom_call_target="tpu_custom_call" | custom-call | flops 1400000000 | bytes 18000000 | tf_op jit(solution)/shard_map/inverse/pallas_call | solution.py:636
Async XLA Ops:
  0.6 172.0 %copy-start.2 = (bf16[2,384,192]{2,1,0:T(8,128)(2,1)S(1)}, bf16[2,384,192]{2,1,0:T(8,128)(2,1)}, u32[]{:S(2)}) copy-start(bf16[2,384,192]{2,1,0:T(8,128)(2,1)} %constant.9.clone.twt_ref) | copy-start | bytes 884740
  172.6 2.0 %copy-start = (bf16[3,8,4,48,384]{4,3,2,1,0:T(8,128)(2,1)S(1)}, bf16[3,8,4,48,384]{4,3,2,1,0:T(8,128)(2,1)}, u32[]{:S(2)}) copy-start(bf16[3,8,4,48,384]{4,3,2,1,0:T(8,128)(2,1)} %get-tuple-element.7.back_ref) | copy-start | bytes 10616836
  174.6 1.1 copy-start.1
  175.7 0.7 copy-start.3

commit v3 on v2

--- a/solution.py
+++ b/solution.py
@@ -18,6 +18,7 @@
 NY = 4
 NZ = 4
 SUB = 2 * GH
+WAVES = 2 * KW // NJ
 BLK = NG * SUB
 QROWS = 4 * BLK
 SPEC_ROWS = 4 * NLAT * KW
@@ -99,10 +100,8 @@
     fbuf,
     cbuf,
     ps,
-    xs_f,
-    xs_g,
-    xr_f,
-    xr_g,
+    xs,
+    xr,
     ys,
     yr,
     yb,
@@ -208,12 +207,12 @@
             bias_ref[:, pl.ds(r * CH, CH)] = bias[r : r + 1]
 
     def x_refs(slot, d, frm):
-        kind, i = slot // 3, slot % 3
-        if kind == 0:
-            return xs_f.at[i, d], xr_f.at[i, frm]
-        if kind == 1:
-            return xs_g.at[i, d], xr_g.at[i, frm]
-        return yrb.at[i, :, pl.ds(pl.multiple_of(lax.rem(d, 4) * BLK, BLK), BLK)], back_hbm.at[i, frm]
+        if slot >= 9:
+            return xs.at[0, 0, d, slot - 9], xr.at[0, 0, frm, slot - 9]
+        if slot < 6:
+            return xs.at[slot % 2, slot // 2, d], xr.at[slot % 2, slot // 2, frm]
+        rows = pl.ds(pl.multiple_of(lax.rem(d, 4) * BLK, BLK), BLK)
+        return yrb.at[slot - 6, :, rows], back_hbm.at[slot - 6, frm]
 
     def x_copy(slot, d, frm):
         src, dst = x_refs(slot, d, frm)
@@ -251,10 +250,9 @@
             x_copy(slot, lax.rem(me + i, ND), me).wait_send()
 
     def y_refs(slot, yy, frm):
-        kind, j = slot // 3, slot % 3
-        if kind < 2:
-            return ys.at[kind, j, yy], yr.at[kind, j, frm]
-        return yb.at[j, yy], yrb.at[j, frm]
+        if slot < 6:
+            return ys.at[slot % 2, slot // 2, yy], yr.at[slot % 2, slot // 2, frm]
+        return yb.at[slot - 6, yy], yrb.at[slot - 6, frm]
 
     def y_copy(slot, yy, frm):
         src, dst = y_refs(slot, yy, frm)
@@ -291,51 +289,43 @@
         def _(i):
             y_copy(slot, lax.rem(y + i, NY), y).wait_send()
 
-    def lon_group(which, g):
+    def lon_group(which, j, g):
         buf = (fbuf, cbuf)[which]
-
-        @pl.loop(0, GH)
-        def _(h):
-            part = dot(tw_ref[xhi], buf[g * GH + h])
+        left = tw_ref[xhi, pl.ds(j * WAVES, WAVES), :]
+        for h in range(GH):
+            part = dot(left, buf[g * GH + h])
             for ct in range(3):
-                ps[ct, pl.ds(pl.multiple_of(h * 2 * KW, 2 * KW), 2 * KW), :] = part[
-                    :, ct * 128 : (ct + 1) * 128
-                ]
-
-        @pl.loop(0, NJ * ND)
-        def _(jd):
-            j, d = jd // ND, lax.rem(jd, ND)
+                ps[ct, pl.ds(h * WAVES, WAVES), :] = part[:, ct * 128 : (ct + 1) * 128]
+        for d in range(ND):
             for ky in range(NY):
-                base = jd * (2 * NY) + 2 * ky
+                base = (d * NY + ky) * 2
                 for ct in range(3):
-                    cols = pl.ds(ct * 128, 128)
                     tile = jnp.concatenate(
-                        [ps[ct, pl.ds(base + r, GH, stride=2 * KW), :] for r in range(2)], 0
+                        [ps[ct, pl.ds(base + r, GH, stride=WAVES), :] for r in range(2)], 0
                     )
-                    tile = (tile * LON_NORM).astype(BF16)
-                    if which == 0:
-                        xs_f[g, d, j * NY + ky, :, cols] = tile
-                    else:
-                        xs_g[j, d, ky, pl.ds(g * SUB, SUB), cols] = tile
-
-    def x_sum_fields(j):
+                    xs[which, j, d, g, ky, :, pl.ds(ct * 128, 128)] = (tile * LON_NORM).astype(BF16)
+
+    def lon_chunk(which, j):
+        @pl.loop(0, NG)
+        def _(g):
+            lon_group(which, j, g)
+
+        x_start(2 * j + which)
+
+    def x_sum(which, j):
         @pl.loop(0, 4)
         def _(s):
-            for ky in range(NY):
-                for g in range(NG):
-                    both = xr_f[g, s, j * NY + ky].astype(F32) + xr_f[g, s + 4, j * NY + ky].astype(
-                        F32
-                    )
+            for g in range(NG):
+                for ky in range(NY):
+                    both = xr[which, j, s, g, ky].astype(F32) + xr[which, j, s + 4, g, ky].astype(F32)
                     rows = pl.ds(pl.multiple_of(s * BLK + g * SUB, SUB), SUB)
-                    ys[0, j, ky, rows, :] = both.astype(BF16)
-
-    def x_sum_cot(j):
-        @pl.loop(0, 4)
-        def _(s):
-            for ky in range(NY):
-                both = xr_g[j, s, ky].astype(F32) + xr_g[j, s + 4, ky].astype(F32)
-                rows = pl.ds(pl.multiple_of(s * BLK, BLK), BLK)
-                ys[1, j, ky, rows, :] = both.astype(BF16)
+                    ys[which, j, ky, rows, :] = both.astype(BF16)
+
+    def x_to_y(which, j):
+        for slot in (9, 10, 11) if which == j == 0 else (2 * j + which,):
+            x_wait_recv(slot)
+        x_sum(which, j)
+        y_start(2 * j + which)
 
     TILE = 192
 
@@ -443,7 +433,7 @@
         gzr[dp] = gz[dp]
         grad_start(0)
 
-    def grad_finish():
+    def grad_finish(after_exchange_starts):
         part = BS // NY
         grad_wait(0)
         total = gzr[0] + gzr[1] + gzr[2] + gzr[3]
@@ -456,6 +446,7 @@
         gd[...] = gyr[0] + gyr[1] + gyr[2] + gyr[3]
         gdr[me] = gd[...]
         grad_start(2)
+        after_exchange_starts()
         grad_wait(2)
         total = gdr[0]
         for i in range(1, ND):
@@ -471,56 +462,36 @@
         gout_ref[...] = gzo[...]
 
     weights_start()
+    for g in range(NG):
+        load(0, g).wait()
+        lon_group(0, 0, g)
+        x_start(9 + g)
+    for g in range(NG):
+        load(1, g).wait()
+    lon_chunk(1, 0)
     gacc[...] = jnp.zeros_like(gacc)
     gb_ref[...] = jnp.zeros_like(gb_ref)
-
-    for g in range(NG):
-        load(0, g).wait()
-        lon_group(0, g)
-        x_start(g)
-    for g in range(NG):
-        load(1, g).wait()
-        lon_group(1, g)
+    for j in range(1, NJ):
+        lon_chunk(0, j)
+        lon_chunk(1, j)
     weights_build()
-    x_wait_recv(0)
-    x_wait_recv(1)
-    x_start(3)
-    x_wait_recv(2)
-    x_start(4)
+
     for j in range(NJ):
-        x_sum_fields(j)
-        y_start(j)
-
-    x_wait_recv(3)
-    x_start(5)
-    x_sum_cot(0)
-    y_start(3)
-    for j in range(NJ):
-        y_wait_recv(j)
-    y_wait_recv(3)
-    spectral(0)
-    x_wait_recv(4)
-    x_sum_cot(1)
-    y_start(4)
-    y_wait_recv(6)
-    x_start(6)
-    y_wait_recv(4)
-    spectral(1)
-    x_wait_recv(5)
-    x_sum_cot(2)
-    y_start(5)
-    y_wait_recv(7)
-    x_start(7)
-    y_wait_recv(5)
-    spectral(2)
+        x_to_y(0, j)
+        x_to_y(1, j)
+        if j > 0:
+            y_wait_recv(5 + j)
+            x_start(5 + j)
+        y_wait_recv(2 * j)
+        y_wait_recv(2 * j + 1)
+        spectral(j)
     grad_begin()
-    y_wait_recv(8)
-    x_start(8)
-    grad_finish()
+    grad_finish(lambda: (y_wait_recv(8), x_start(8)))
+    for slot in range(6, 9):
+        x_wait_recv(slot)
+    for slot in range(1, 12):
+        x_wait_send(slot)
     for slot in range(9):
-        if slot >= 6:
-            x_wait_recv(slot)
-        x_wait_send(slot)
         y_wait_send(slot)
 
 
@@ -555,11 +526,9 @@
             pltpu.VMEM((NZ, NY, BS // NY, CH), F32),
             pltpu.VMEM((ROWS, HALF, CH), BF16),
             pltpu.VMEM((ROWS, HALF, CH), BF16),
-            pltpu.VMEM((3, GH * 2 * KW, 128), F32),
-            pltpu.VMEM((NG, ND, NJ * NY, SUB, CH), BF16),
-            pltpu.VMEM((NJ, ND, NY, BLK, CH), BF16),
-            pltpu.VMEM((NG, ND, NJ * NY, SUB, CH), BF16),
-            pltpu.VMEM((NJ, ND, NY, BLK, CH), BF16),
+            pltpu.VMEM((3, GH * WAVES, 128), F32),
+            pltpu.VMEM((2, NJ, ND, NG, NY, SUB, CH), BF16),
+            pltpu.VMEM((2, NJ, ND, NG, NY, SUB, CH), BF16),
             pltpu.VMEM((2, NJ, NY, QROWS, CH), BF16),
             pltpu.VMEM((2, NJ, NY, QROWS, CH), BF16),
             pltpu.VMEM((NJ, NY, QROWS, CH), BF16),
@@ -571,9 +540,9 @@
             pltpu.VMEM((NLAT, 2 * CH), F32),
             pltpu.VMEM((2 * NLAT, CH), BF16),
             dma((2, NG)),
-            dma((9,)),
-            dma((9, ND)),
-            dma((9, ND)),
+            dma((12,)),
+            dma((12, ND)),
+            dma((12, ND)),
             dma((9,)),
             dma((9, NY)),
             dma((9, NY)),
@@ -656,7 +625,7 @@
             whole(2, 2, BS),
         ),
         scratch_shapes=[pltpu.VMEM((3, GH * 2 * KW, 128), F32)],
-        compiler_params=pltpu.CompilerParams(vmem_limit_bytes=48 << 20),
+        compiler_params=pltpu.CompilerParams(vmem_limit_bytes=62 << 20),
         cost_estimate=pl.CostEstimate(
             flops=1400 * 10**6, bytes_accessed=18 * 10**6, transcendentals=0
         ),

time: 191 us -> 166 us (0.87)
  Pallas kernels: 186 us -> 165 us
  local copies, waits for them, and re-layouts: 3.77 us -> 0 us
    pallas_call x1, Pallas kernels: 172 us -> 151 us  [spectral_call(): pl.pallas_call(spectral_kernel, out_shape=(jax.ShapeDtypeStruct((NJ, ND,...]
    unnamed x8 -> x0, local copies, waits for them, and re-layouts: 3.77 us -> none
where the time goes in v3:
time: 166 us
  Pallas kernels  165 us (99%)
    pallas_call x1, Pallas kernels, spectral_call(): pl.pallas_call(spectral_kernel, out_shape=(jax.ShapeDtypeStruct((NJ, ND,...  151 us
    pallas_call x1, Pallas kernels, inverse_call(): pl.pallas_call(inverse_kernel, grid=(NG,), out_shape=(jax.ShapeDtypeStruc...  14.2 us

profile of v3, /device:TPU:1, one launch (start us, length us, event | category | flops | bytes accessed | tf_op | source)
XLA Modules:
  0.0 165.5 jit_solution(2841222994686583113)
XLA Ops:
  0.6 150.5 %spectral.1 = (bf16[3,8,4,48,384]{4,3,2,1,0:T(8,128)(2,1)}, f32[4,4,24,384]{3,2,1,0:T(8,128)}, f32[8,384]{1,0:T(8,128)}) custom-call(bf16[1,24,384,384]{3,2,1,0:T(8,128)(2,1)} %f_hbm.1, bf16[1,24,384,384]{3,2,1,0:T(8,128)(2,1)} %cot_ref.1, bf16[2,192,384]{2,1,0:T(8,128)(2,1)} %constant.8.clone.tw_ref, bf16[768,768]{1,0:T(8,128)(2,1)} %constant.10.clone.th_ref, ...), custom_call_target="tpu_custom_call" | custom-call | flops 10000000000 | bytes 30000000 | tf_op jit(solution)/shard_map/spectral/pallas_call | solution.py:502
  151.2 14.2 %inverse.1 = (bf16[1,24,384,384]{3,2,1,0:T(8,128)(2,1)}, f32[2,2,96,96]{3,2,1,0:T(8,128)}, f32[2,2,96,96]{3,2,1,0:T(8,128)}, f32[2,2,96]{2,1,0:T(2,128)}) custom-call(bf16[3,8,4,48,384]{4,3,2,1,0:T(8,128)(2,1)} %get-tuple-element.7.back_ref, bf16[1,24,384,384]{3,2,1,0:T(8,128)(2,1)} %cot_ref.1, bf16[2,384,192]{2,1,0:T(8,128)(2,1)} %constant.9.clone.twt_ref, ...), custom_call_target="tpu_custom_call" | custom-call | flops 1400000000 | bytes 18000000 | tf_op jit(solution)/shard_map/inverse/pallas_call | solution.py:605

commit v4 on v3

--- a/solution.py
+++ b/solution.py
@@ -17,6 +17,7 @@
 ND = 8
 NY = 4
 NZ = 4
+LANES = 256
 SUB = 2 * GH
 WAVES = 2 * KW // NJ
 BLK = NG * SUB
@@ -207,12 +208,13 @@
             bias_ref[:, pl.ds(r * CH, CH)] = bias[r : r + 1]
 
     def x_refs(slot, d, frm):
-        if slot >= 9:
-            return xs.at[0, 0, d, slot - 9], xr.at[0, 0, frm, slot - 9]
+        if slot >= 15:
+            return xs.at[0, 0, d, slot - 15], xr.at[0, 0, frm, slot - 15]
         if slot < 6:
             return xs.at[slot % 2, slot // 2, d], xr.at[slot % 2, slot // 2, frm]
-        rows = pl.ds(pl.multiple_of(lax.rem(d, 4) * BLK, BLK), BLK)
-        return yrb.at[slot - 6, :, rows], back_hbm.at[slot - 6, frm]
+        j, g = (slot - 6) // NG, (slot - 6) % NG
+        rows = pl.ds(pl.multiple_of(lax.rem(d, 4) * BLK + g * SUB, SUB), SUB)
+        return yrb.at[j, :, rows], back_hbm.at[g, j, frm]
 
     def x_copy(slot, d, frm):
         src, dst = x_refs(slot, d, frm)
@@ -296,7 +298,9 @@
             part = dot(left, buf[g * GH + h])
             for ct in range(3):
                 ps[ct, pl.ds(h * WAVES, WAVES), :] = part[:, ct * 128 : (ct + 1) * 128]
-        for d in range(ND):
+
+        @pl.loop(0, ND)
+        def _(d):
             for ky in range(NY):
                 base = (d * NY + ky) * 2
                 for ct in range(3):
@@ -322,7 +326,7 @@
                     ys[which, j, ky, rows, :] = both.astype(BF16)
 
     def x_to_y(which, j):
-        for slot in (9, 10, 11) if which == j == 0 else (2 * j + which,):
+        for slot in (15, 16, 17) if which == j == 0 else (2 * j + which,):
             x_wait_recv(slot)
         x_sum(which, j)
         y_start(2 * j + which)
@@ -368,24 +372,26 @@
                 trows = pl.ds(pl.multiple_of(q * NLAT + t * TILE, TILE), TILE)
                 dsbuf[trows, :] = ds[:, q * CH : (q + 1) * CH]
 
+        re, im = pl.ds(0, CH), pl.ds(CH, CH)
+        for i, (zz, dd) in enumerate(((zbuf, dzbuf), (hbuf, dobuf))):
+            gacc[2 * i] += dot_tn(zz[:, re], dd[:, re]) + dot_tn(zz[:, im], dd[:, im])
+            gacc[2 * i + 1] += dot_tn(zz[:, re], dd[:, im]) - dot_tn(zz[:, im], dd[:, re])
+        if j == NJ - 1:
+            grad_begin()
+
         @pl.loop(0, NY)
         def _(yy):
             rows = pl.ds(pl.multiple_of(yy * QROWS, QROWS), QROWS)
             yb[j, yy] = (dot(tht_ref[rows, :], dsbuf[...]) * LAT_NORM).astype(BF16)
 
         y_start(6 + j)
-
-        re, im = pl.ds(0, CH), pl.ds(CH, CH)
-        for i, (zz, dd) in enumerate(((zbuf, dzbuf), (hbuf, dobuf))):
-            gacc[2 * i] += dot_tn(zz[:, re], dd[:, re]) + dot_tn(zz[:, im], dd[:, im])
-            gacc[2 * i + 1] += dot_tn(zz[:, re], dd[:, im]) - dot_tn(zz[:, im], dd[:, re])
 
     def grad_copy(stage, to, frm):
         src, dst, target = (
             lambda: (gz.at[to], gzr.at[frm], device(y, me, to)),
             lambda: (gy.at[to], gyr.at[frm], device(to, me)),
             lambda: (gd, gdr.at[frm], device(y, to)),
-            lambda: (gd.at[pl.ds(0, BS // NY)], gyo.at[frm], device(to, me)),
+            lambda: (gd.at[pl.ds(0, BS // NY), lanes], gyo.at[frm], device(to, me)),
             lambda: (gyo, gzo.at[frm], device(y, me, to)),
         )[stage]()
         return pltpu.make_async_remote_copy(
@@ -397,6 +403,7 @@
             device_id_type=MESH,
         )
 
+    lanes = pl.ds(pl.multiple_of(xhi * 128, 128), LANES)
     stage_size = (NZ, NY, ND, NY, NZ)
     stage_place = (dp, y, me, y, dp)
 
@@ -433,7 +440,7 @@
         gzr[dp] = gz[dp]
         grad_start(0)
 
-    def grad_finish(after_exchange_starts):
+    def grad_finish(before_exchange, after_exchange_starts):
         part = BS // NY
         grad_wait(0)
         total = gzr[0] + gzr[1] + gzr[2] + gzr[3]
@@ -442,6 +449,7 @@
             gy[i, pl.ds(part, 8), :] = total[BS:]
         gyr[y] = gy[y]
         grad_start(1)
+        before_exchange()
         grad_wait(1)
         gd[...] = gyr[0] + gyr[1] + gyr[2] + gyr[3]
         gdr[me] = gd[...]
@@ -452,8 +460,8 @@
         for i in range(1, ND):
             total += gdr[i]
         gd[...] = total
-        gbout_ref[...] = total[part:]
-        gyo[y] = total[:part]
+        gbout_ref[...] = gd[pl.ds(part, 8), lanes]
+        gyo[y] = gd[pl.ds(0, part), lanes]
         grad_start(3)
         grad_wait(3)
         gzo[dp] = gyo[...]
@@ -465,7 +473,7 @@
     for g in range(NG):
         load(0, g).wait()
         lon_group(0, 0, g)
-        x_start(9 + g)
+        x_start(15 + g)
     for g in range(NG):
         load(1, g).wait()
     lon_chunk(1, 0)
@@ -481,15 +489,21 @@
         x_to_y(1, j)
         if j > 0:
             y_wait_recv(5 + j)
-            x_start(5 + j)
+            for g in range(NG if j < NJ - 1 else NG - 1):
+                x_start(6 + (j - 1) * NG + g)
         y_wait_recv(2 * j)
         y_wait_recv(2 * j + 1)
         spectral(j)
-    grad_begin()
-    grad_finish(lambda: (y_wait_recv(8), x_start(8)))
-    for slot in range(6, 9):
+
+    def last_return():
+        y_wait_recv(8)
+        for g in range(NG):
+            x_start(12 + g)
+
+    grad_finish(lambda: x_start(11), last_return)
+    for slot in range(6, 15):
         x_wait_recv(slot)
-    for slot in range(1, 12):
+    for slot in range(1, 18):
         x_wait_send(slot)
     for slot in range(9):
         y_wait_send(slot)
@@ -502,9 +516,9 @@
     return pl.pallas_call(
         spectral_kernel,
         out_shape=(
-            jax.ShapeDtypeStruct((NJ, ND, NY, BLK, CH), BF16),
-            jax.ShapeDtypeStruct((NZ, NY, BS // NY, CH), F32),
-            jax.ShapeDtypeStruct((8, CH), F32),
+            jax.ShapeDtypeStruct((NG, NJ, ND, NY, SUB, CH), BF16),
+            jax.ShapeDtypeStruct((NZ, NY, BS // NY, LANES), F32),
+            jax.ShapeDtypeStruct((8, LANES), F32),
         ),
         in_specs=[hbm, hbm] + [vm] * 6,
         out_specs=(hbm, vm, vm),
@@ -522,8 +536,8 @@
             pltpu.VMEM((NY, BS // NY + 8, CH), F32),
             pltpu.VMEM((BS // NY + 8, CH), F32),
             pltpu.VMEM((ND, BS // NY + 8, CH), F32),
-            pltpu.VMEM((NY, BS // NY, CH), F32),
-            pltpu.VMEM((NZ, NY, BS // NY, CH), F32),
+            pltpu.VMEM((NY, BS // NY, LANES), F32),
+            pltpu.VMEM((NZ, NY, BS // NY, LANES), F32),
             pltpu.VMEM((ROWS, HALF, CH), BF16),
             pltpu.VMEM((ROWS, HALF, CH), BF16),
             pltpu.VMEM((3, GH * WAVES, 128), F32),
@@ -540,9 +554,9 @@
             pltpu.VMEM((NLAT, 2 * CH), F32),
             pltpu.VMEM((2 * NLAT, CH), BF16),
             dma((2, NG)),
-            dma((12,)),
-            dma((12, ND)),
-            dma((12, ND)),
+            dma((18,)),
+            dma((18, ND)),
+            dma((18, ND)),
             dma((9,)),
             dma((9, NY)),
             dma((9, NY)),
@@ -560,71 +574,125 @@
     )(fields, cotangent, tw, th, tht, w_first, w_second, bias)
 
 
-def inverse_kernel(back_ref, cot_ref, twt_ref, grad_ref, bias_ref, out_ref, g1_ref, g2_ref, gb_ref, bs):
+PAIR = 2
+TILE_W = 128
+
+
+def inverse_kernel(
+    back_hbm,
+    cot_hbm,
+    twt_hbm,
+    grad_ref,
+    bias_ref,
+    out_hbm,
+    g1_ref,
+    g2_ref,
+    gb_ref,
+    bs,
+    back,
+    buf,
+    twt,
+    back_sem,
+    cot_sem,
+    out_sem,
+    twt_sem,
+):
     xhi = lax.axis_index("lon")
 
-    @pl.loop(0, NJ * ND)
-    def _(jd):
-        j, d = jd // ND, lax.rem(jd, ND)
-        for ky in range(NY):
-            rows = pl.ds(pl.multiple_of(jd * NY * SUB + ky * SUB, SUB), SUB)
-            for ct in range(3):
-                bs[ct, rows, :] = back_ref[j, d, ky, :, pl.ds(ct * 128, 128)].astype(F32)
-
-    @pl.loop(0, GH)
-    def _(h):
-        spec = jnp.concatenate(
-            [bs[ct, pl.ds(h, 2 * KW, stride=GH), :].astype(BF16) for ct in range(3)], 1
-        )
-        spatial = dot(twt_ref[xhi], spec) * LON_NORM
-        out_ref[0, h] = (cot_ref[0, h].astype(F32) + spatial).astype(BF16)
-
-    @pl.when(pl.program_id(0) == 0)
-    def _():
-        scale = 1.0 / math.sqrt(SPEC_ROWS)
-        row = lax.broadcasted_iota(jnp.int32, (CH, BS), 0)
-        col = lax.broadcasted_iota(jnp.int32, (CH, BS), 1)
-        for m in range(2):
-            pick = (row == col + (2 * xhi + m) * BS).astype(F32)
-
-            def take(value):
-                return scale * jnp.dot(
-                    value, pick, precision=lax.Precision.HIGHEST, preferred_element_type=F32
-                )
-
-            for r in range(2):
-                g1_ref[m, r] = take(grad_ref[r].reshape(BS, CH))
-                g2_ref[m, r] = take(grad_ref[2 + r].reshape(BS, CH))
-            gb_ref[m] = take(bias_ref[...])[:2]
+    def load_back(g):
+        return pltpu.make_async_copy(back_hbm.at[g], back.at[g], back_sem.at[g])
+
+    def load_cot(g):
+        rows = pl.ds(g * GH, GH)
+        return pltpu.make_async_copy(cot_hbm.at[0, rows], buf.at[rows], cot_sem.at[g])
+
+    def store(i):
+        rows = pl.ds(i * PAIR, PAIR)
+        return pltpu.make_async_copy(buf.at[rows], out_hbm.at[0, rows], out_sem.at[i])
+
+    table = pltpu.make_async_copy(twt_hbm.at[xhi], twt, twt_sem.at[0])
+    for g in range(NG):
+        load_back(g).start()
+        if g == 0:
+            table.start()
+        load_cot(g).start()
+
+    scale = 1.0 / math.sqrt(SPEC_ROWS)
+    row = lax.broadcasted_iota(jnp.int32, (LANES, BS), 0)
+    col = lax.broadcasted_iota(jnp.int32, (LANES, BS), 1)
+    for m in range(2):
+        pick = (row == col + (xhi * 64 + m * BS)).astype(F32)
+
+        def take(value):
+            return scale * jnp.dot(
+                value, pick, precision=lax.Precision.HIGHEST, preferred_element_type=F32
+            )
+
+        for r in range(2):
+            g1_ref[m, r] = take(grad_ref[r].reshape(BS, LANES))
+            g2_ref[m, r] = take(grad_ref[2 + r].reshape(BS, LANES))
+        gb_ref[m] = take(bias_ref[...])[:2]
+    table.wait()
+
+    @pl.loop(0, NG)
+    def _(g):
+        load_back(g).wait()
+
+        @pl.loop(0, NJ * ND)
+        def _(jd):
+            j, d = jd // ND, lax.rem(jd, ND)
+            for ky in range(NY):
+                rows = pl.ds(pl.multiple_of(jd * NY * SUB + ky * SUB, SUB), SUB)
+                for ct in range(3):
+                    bs[ct, rows, :] = back[g, j, d, ky, :, pl.ds(ct * 128, 128)].astype(F32)
+
+        load_cot(g).wait()
+        for hp in range(GH // PAIR):
+            spec = jnp.concatenate(
+                [
+                    bs[ct, pl.ds(hp * PAIR + k, 2 * KW, stride=GH), :].astype(BF16)
+                    for k in range(PAIR)
+                    for ct in range(3)
+                ],
+                1,
+            )
+            for t in range(HALF // TILE_W):
+                cols = pl.ds(t * TILE_W, TILE_W)
+                part = dot(twt[cols, :], spec) * LON_NORM
+                for k in range(PAIR):
+                    h = g * GH + hp * PAIR + k
+                    value = buf[h, cols].astype(F32) + part[:, k * CH : (k + 1) * CH]
+                    buf[h, cols] = value.astype(BF16)
+            store(g * (GH // PAIR) + hp).start()
+
+    for i in range(ROWS // PAIR):
+        store(i).wait()
 
 
 def inverse_call(back, cotangent, twt, grads, bias):
-    def whole(*shape):
-        return pl.BlockSpec(shape, lambda g: (0,) * len(shape))
-
+    vm = pl.BlockSpec(memory_space=pltpu.VMEM)
+    hbm = pl.BlockSpec(memory_space=pl.ANY)
+    dma = pltpu.SemaphoreType.DMA
     return pl.pallas_call(
         inverse_kernel,
-        grid=(NG,),
         out_shape=(
             jax.ShapeDtypeStruct((1, ROWS, HALF, CH), BF16),
             jax.ShapeDtypeStruct((2, 2, BS, BS), F32),
             jax.ShapeDtypeStruct((2, 2, BS, BS), F32),
             jax.ShapeDtypeStruct((2, 2, BS), F32),
         ),
-        in_specs=[
-            pl.BlockSpec((NJ, ND, NY, SUB, CH), lambda g: (0, 0, 0, g, 0)),
-            pl.BlockSpec((1, GH, HALF, CH), lambda g: (0, g, 0, 0)),
-            whole(2, HALF, 2 * KW),
-            whole(NZ, NY, BS // NY, CH),
-            whole(8, CH),
+        in_specs=[hbm, hbm, hbm, vm, vm],
+        out_specs=(hbm, vm, vm, vm),
+        scratch_shapes=[
+            pltpu.VMEM((3, GH * 2 * KW, 128), F32),
+            pltpu.VMEM((NG, NJ, ND, NY, SUB, CH), BF16),
+            pltpu.VMEM((ROWS, HALF, CH), BF16),
+            pltpu.VMEM((HALF, 2 * KW), BF16),
+            dma((NG,)),
+            dma((NG,)),
+            dma((ROWS // PAIR,)),
+            dma((1,)),
         ],
-        out_specs=(
-            pl.BlockSpec((1, GH, HALF, CH), lambda g: (0, g, 0, 0)),
-            whole(2, 2, BS, BS),
-            whole(2, 2, BS, BS),
-            whole(2, 2, BS),
-        ),
-        scratch_shapes=[pltpu.VMEM((3, GH * 2 * KW, 128), F32)],
         compiler_params=pltpu.CompilerParams(vmem_limit_bytes=62 << 20),
         cost_estimate=pl.CostEstimate(
             flops=1400 * 10**6, bytes_accessed=18 * 10**6, transcendentals=0

time: 166 us -> 165 us (level)
  no operation moved by 1% of the time
where the time goes in v4:
time: 165 us; the launch traced here: 164 us
  Pallas kernels  164 us (99%)
    pallas_call x1, Pallas kernels, spectral_call(): pl.pallas_call(spectral_kernel, out_shape=(jax.ShapeDtypeStruct((NG, NJ,...  152 us
    pallas_call x1, Pallas kernels, inverse_call(): pl.pallas_call(inverse_kernel, out_shape=(jax.ShapeDtypeStruct((1, ROWS,...  11.7 us

profile of v4, /device:TPU:1, one launch (start us, length us, event | category | flops | bytes accessed | tf_op | source)
XLA Modules:
  0.0 164.5 jit_solution(14470916014529650032)
XLA Ops:
  0.6 152.0 %spectral.1 = (bf16[3,3,8,4,16,384]{5,4,3,2,1,0:T(8,128)(2,1)}, f32[4,4,24,256]{3,2,1,0:T(8,128)}, f32[8,256]{1,0:T(8,128)}) custom-call(bf16[1,24,384,384]{3,2,1,0:T(8,128)(2,1)} %f_hbm.1, bf16[1,24,384,384]{3,2,1,0:T(8,128)(2,1)} %cot_hbm.1, bf16[2,192,384]{2,1,0:T(8,128)(2,1)} %constant.8.clone.tw_ref, bf16[768,768]{1,0:T(8,128)(2,1)} %constant.10.clone.th_ref, ...), custom_call_target="tpu_custom_call" | custom-call | flops 10000000000 | bytes 30000000 | tf_op jit(solution)/shard_map/spectral/pallas_call | solution.py:516
  152.6 11.7 %inverse.1 = (bf16[1,24,384,384]{3,2,1,0:T(8,128)(2,1)}, f32[2,2,96,96]{3,2,1,0:T(8,128)}, f32[2,2,96,96]{3,2,1,0:T(8,128)}, f32[2,2,96]{2,1,0:T(2,128)}) custom-call(bf16[3,3,8,4,16,384]{5,4,3,2,1,0:T(8,128)(2,1)} %get-tuple-element.7.back_hbm, bf16[1,24,384,384]{3,2,1,0:T(8,128)(2,1)} %cot_hbm.1, bf16[2,384,192]{2,1,0:T(8,128)(2,1)} %constant.9.clone.twt_hbm, ...), custom_call_target="tpu_custom_call" | custom-call | flops 1400000000 | bytes 18000000 | tf_op jit(solution)/shard_map/inverse/pallas_call | solution.py:676

commit v5 on v4

--- a/solution.py
+++ b/solution.py
@@ -74,9 +74,9 @@
 def spectral_kernel(
     f_hbm,
     c_hbm,
-    tw_ref,
-    th_ref,
-    tht_ref,
+    tw_hbm,
+    th_hbm,
+    tht_hbm,
     w1_ref,
     w2_ref,
     b1_ref,
@@ -97,9 +97,12 @@
     gd,
     gdr,
     gyo,
+    gzs,
     gzo,
+    tw_ref,
+    th_ref,
+    tht_ref,
     fbuf,
-    cbuf,
     ps,
     xs,
     xr,
@@ -111,9 +114,11 @@
     hbuf,
     dobuf,
     dzbuf,
-    gmbuf,
+    slope,
+    keep,
     dsbuf,
     ld_sem,
+    table_sem,
     xl_sem,
     xsend,
     xrecv,
@@ -136,13 +141,17 @@
         return (zz, yy * 4 + lax.rem(d, 4), d // 4)
 
     def load(which, g):
-        src, dst = ((f_hbm, fbuf), (c_hbm, cbuf))[which]
+        src = (f_hbm, c_hbm)[which]
         rows = pl.ds(g * GH, GH)
-        return pltpu.make_async_copy(src.at[0, rows], dst.at[rows], ld_sem.at[which, g])
-
-    for which in range(2):
-        for g in range(NG):
-            load(which, g).start()
+        return pltpu.make_async_copy(src.at[0, rows], fbuf.at[rows], ld_sem.at[which, g])
+
+    def load_table(i):
+        src = (tw_hbm.at[xhi], th_hbm, tht_hbm)[i]
+        return pltpu.make_async_copy(src, (tw_ref, th_ref, tht_ref)[i], table_sem.at[i])
+
+    load_table(0).start()
+    for g in range(NG):
+        load(0, g).start()
 
     barrier = pltpu.get_barrier_semaphore()
     for i in range(1, ND):
@@ -211,7 +220,7 @@
         if slot >= 15:
             return xs.at[0, 0, d, slot - 15], xr.at[0, 0, frm, slot - 15]
         if slot < 6:
-            return xs.at[slot % 2, slot // 2, d], xr.at[slot % 2, slot // 2, frm]
+            return xs.at[slot // NJ, slot % NJ, d], xr.at[slot // NJ, slot % NJ, frm]
         j, g = (slot - 6) // NG, (slot - 6) % NG
         rows = pl.ds(pl.multiple_of(lax.rem(d, 4) * BLK + g * SUB, SUB), SUB)
         return yrb.at[j, :, rows], back_hbm.at[g, j, frm]
@@ -253,7 +262,7 @@
 
     def y_refs(slot, yy, frm):
         if slot < 6:
-            return ys.at[slot % 2, slot // 2, yy], yr.at[slot % 2, slot // 2, frm]
+            return ys.at[slot // NJ, slot % NJ, yy], yr.at[slot // NJ, slot % NJ, frm]
         return yb.at[slot - 6, yy], yrb.at[slot - 6, frm]
 
     def y_copy(slot, yy, frm):
@@ -292,10 +301,9 @@
             y_copy(slot, lax.rem(y + i, NY), y).wait_send()
 
     def lon_group(which, j, g):
-        buf = (fbuf, cbuf)[which]
-        left = tw_ref[xhi, pl.ds(j * WAVES, WAVES), :]
+        left = tw_ref[pl.ds(j * WAVES, WAVES), :]
         for h in range(GH):
-            part = dot(left, buf[g * GH + h])
+            part = dot(left, fbuf[g * GH + h])
             for ct in range(3):
                 ps[ct, pl.ds(h * WAVES, WAVES), :] = part[:, ct * 128 : (ct + 1) * 128]
 
@@ -314,8 +322,6 @@
         def _(g):
             lon_group(which, j, g)
 
-        x_start(2 * j + which)
-
     def x_sum(which, j):
         @pl.loop(0, 4)
         def _(s):
@@ -326,14 +332,36 @@
                     ys[which, j, ky, rows, :] = both.astype(BF16)
 
     def x_to_y(which, j):
-        for slot in (15, 16, 17) if which == j == 0 else (2 * j + which,):
+        for slot in (15, 16, 17) if which == j == 0 else (NJ * which + j,):
             x_wait_recv(slot)
+        if which == 0:
+            x_start(NJ + j)
         x_sum(which, j)
-        y_start(2 * j + which)
+        y_start(NJ * which + j)
 
     TILE = 192
 
-    def spectral(j):
+    def forward(j):
+        @pl.loop(0, 2)
+        def _(t):
+            rows = pl.ds(pl.multiple_of(t * TILE, TILE), TILE)
+            for q in range(2):
+                trows = pl.ds(pl.multiple_of(q * NLAT + t * TILE, TILE), TILE)
+                zbuf[j, rows, pl.ds(q * CH, CH)] = (
+                    dot(th_ref[trows, :], yr[0, j].reshape(2 * NLAT, CH)) * LAT_NORM
+                ).astype(BF16)
+            o1 = dot(zbuf[j, rows, :], wc1_ref[...]) + bias_ref[...]
+            square = o1 * o1
+            tangent = jnp.tanh(root * (o1 + gelu_coef * o1 * square))
+            hbuf[j, rows, :] = (0.5 * o1 * (1.0 + tangent)).astype(BF16)
+            slope[j, rows, :] = 0.5 * (1.0 + tangent) + 0.5 * o1 * (
+                1.0 - tangent * tangent
+            ) * root * (1.0 + 3.0 * gelu_coef * square)
+            o2 = dot(hbuf[j, rows, :], wc2_ref[...])
+            square = o2 * o2
+            keep[j, rows, :] = square / (square + shrink_level * shrink_level)
+
+    def backward(j):
         wave = (j * ND + me) * NY + y
         doubling = jnp.where(wave == 0, 1.0, 2.0).astype(F32) * LAT_NORM
 
@@ -343,28 +371,10 @@
             for q in range(2):
                 trows = pl.ds(pl.multiple_of(q * NLAT + t * TILE, TILE), TILE)
                 cols = pl.ds(q * CH, CH)
-                left = th_ref[trows, :]
-                zbuf[rows, cols] = (
-                    dot(left, yr[0, j].reshape(2 * NLAT, CH)) * LAT_NORM
-                ).astype(BF16)
-                gmbuf[rows, cols] = dot(left, yr[1, j].reshape(2 * NLAT, CH)) * doubling
-
-        @pl.loop(0, 2)
-        def _(t):
-            rows = pl.ds(pl.multiple_of(t * TILE, TILE), TILE)
-            o1 = dot(zbuf[rows, :], wc1_ref[...]) + bias_ref[...]
-            square = o1 * o1
-            tangent = jnp.tanh(root * (o1 + gelu_coef * o1 * square))
-            hbuf[rows, :] = (0.5 * o1 * (1.0 + tangent)).astype(BF16)
-            slope = 0.5 * (1.0 + tangent) + 0.5 * o1 * (1.0 - tangent * tangent) * root * (
-                1.0 + 3.0 * gelu_coef * square
-            )
-            o2 = dot(hbuf[rows, :], wc2_ref[...])
-            square = o2 * o2
-            keep = square / (square + shrink_level * shrink_level)
-            dobuf[rows, :] = (keep * gmbuf[rows, :]).astype(BF16)
+                gm = dot(th_ref[trows, :], yr[1, j].reshape(2 * NLAT, CH)) * doubling
+                dobuf[rows, cols] = (keep[j, rows, cols] * gm).astype(BF16)
             dh = dot_nt(dobuf[rows, :], wc2_ref[...])
-            dz = (slope * dh).astype(BF16)
+            dz = (slope[j, rows, :] * dh).astype(BF16)
             dzbuf[rows, :] = dz
             gb_ref[...] += jnp.sum(dz.astype(F32), 0, keepdims=True)
             ds = dot_nt(dz, wc1_ref[...]).astype(BF16)
@@ -372,19 +382,17 @@
                 trows = pl.ds(pl.multiple_of(q * NLAT + t * TILE, TILE), TILE)
                 dsbuf[trows, :] = ds[:, q * CH : (q + 1) * CH]
 
-        re, im = pl.ds(0, CH), pl.ds(CH, CH)
-        for i, (zz, dd) in enumerate(((zbuf, dzbuf), (hbuf, dobuf))):
-            gacc[2 * i] += dot_tn(zz[:, re], dd[:, re]) + dot_tn(zz[:, im], dd[:, im])
-            gacc[2 * i + 1] += dot_tn(zz[:, re], dd[:, im]) - dot_tn(zz[:, im], dd[:, re])
-        if j == NJ - 1:
-            grad_begin()
-
+    def back(j):
         @pl.loop(0, NY)
         def _(yy):
             rows = pl.ds(pl.multiple_of(yy * QROWS, QROWS), QROWS)
             yb[j, yy] = (dot(tht_ref[rows, :], dsbuf[...]) * LAT_NORM).astype(BF16)
 
-        y_start(6 + j)
+    def weight_grads(j):
+        re, im = pl.ds(0, CH), pl.ds(CH, CH)
+        for i, (zz, dd) in enumerate(((zbuf, dzbuf), (hbuf, dobuf))):
+            gacc[2 * i] += dot_tn(zz[j, :, re], dd[:, re]) + dot_tn(zz[j, :, im], dd[:, im])
+            gacc[2 * i + 1] += dot_tn(zz[j, :, re], dd[:, im]) - dot_tn(zz[j, :, im], dd[:, re])
 
     def grad_copy(stage, to, frm):
         src, dst, target = (
@@ -392,7 +400,7 @@
             lambda: (gy.at[to], gyr.at[frm], device(to, me)),
             lambda: (gd, gdr.at[frm], device(y, to)),
             lambda: (gd.at[pl.ds(0, BS // NY), lanes], gyo.at[frm], device(to, me)),
-            lambda: (gyo, gzo.at[frm], device(y, me, to)),
+            lambda: (gzs, gzo.at[frm], device(y, me, to)),
         )[stage]()
         return pltpu.make_async_remote_copy(
             src_ref=src,
@@ -428,25 +436,27 @@
 
     def grad_begin():
         lane = lax.broadcasted_iota(jnp.int32, (BS, CH), 1)
-        line = lax.broadcasted_iota(jnp.int32, (8, CH), 0)
-        both = [jnp.broadcast_to(gb_ref[:, pl.ds(r * CH, CH)], (8, CH)) for r in range(2)]
+        line = lax.broadcasted_iota(jnp.int32, (SUB, CH), 0)
+        both = [jnp.broadcast_to(gb_ref[:, pl.ds(r * CH, CH)], (SUB, CH)) for r in range(2)]
         sums = jnp.where(line == 0, both[0], jnp.where(line == 1, both[1], 0.0))
         for i in range(NZ):
             part = gacc[i, pl.ds(0, BS), :]
             for n in range(1, NBLK):
                 part = jnp.where(lane >= n * BS, gacc[i, pl.ds(n * BS, BS), :], part)
-            gz[i, pl.ds(0, BS), :] = part
-            gz[i, pl.ds(BS, 8), :] = sums
+            gz[i, pl.ds(0, BS), :] = part.astype(BF16)
+            gz[i, pl.ds(BS, SUB), :] = sums.astype(BF16)
         gzr[dp] = gz[dp]
         grad_start(0)
 
     def grad_finish(before_exchange, after_exchange_starts):
         part = BS // NY
         grad_wait(0)
-        total = gzr[0] + gzr[1] + gzr[2] + gzr[3]
+        total = gzr[0].astype(F32)
+        for i in range(1, NZ):
+            total += gzr[i].astype(F32)
         for i in range(NY):
             gy[i, pl.ds(0, part), :] = total[i * part : (i + 1) * part]
-            gy[i, pl.ds(part, 8), :] = total[BS:]
+            gy[i, pl.ds(part, 8), :] = total[BS : BS + 8]
         gyr[y] = gy[y]
         grad_start(1)
         before_exchange()
@@ -464,36 +474,69 @@
         gyo[y] = gd[pl.ds(0, part), lanes]
         grad_start(3)
         grad_wait(3)
-        gzo[dp] = gyo[...]
+        gzs[...] = gyo[...].reshape(BS, LANES).astype(BF16)
+        gzo[dp] = gzs[...]
         grad_start(4)
         grad_wait(4)
-        gout_ref[...] = gzo[...]
+        gout_ref[...] = gzo[...].astype(F32).reshape(NZ, NY, part, LANES)
 
     weights_start()
+    load_table(0).wait()
     for g in range(NG):
         load(0, g).wait()
         lon_group(0, 0, g)
         x_start(15 + g)
+    for i in range(1, 3):
+        load_table(i).start()
+    for j in range(1, NJ):
+        lon_chunk(0, j)
+        x_start(j)
+    for g in range(NG):
+        load(1, g).start()
+    gacc[...] = jnp.zeros_like(gacc)
+    gb_ref[...] = jnp.zeros_like(gb_ref)
+    weights_build()
     for g in range(NG):
         load(1, g).wait()
     lon_chunk(1, 0)
-    gacc[...] = jnp.zeros_like(gacc)
-    gb_ref[...] = jnp.zeros_like(gb_ref)
+    x_to_y(0, 0)
     for j in range(1, NJ):
-        lon_chunk(0, j)
         lon_chunk(1, j)
-    weights_build()
-
-    for j in range(NJ):
-        x_to_y(0, j)
-        x_to_y(1, j)
-        if j > 0:
-            y_wait_recv(5 + j)
-            for g in range(NG if j < NJ - 1 else NG - 1):
-                x_start(6 + (j - 1) * NG + g)
-        y_wait_recv(2 * j)
-        y_wait_recv(2 * j + 1)
-        spectral(j)
+    x_to_y(0, 1)
+    for i in range(1, 3):
+        load_table(i).wait()
+    for j in range(2):
+        y_wait_recv(j)
+        forward(j)
+    x_to_y(0, 2)
+    y_wait_recv(2)
+    forward(2)
+    x_to_y(1, 0)
+    y_wait_recv(3)
+    backward(0)
+    back(0)
+    x_to_y(1, 1)
+    weight_grads(0)
+    y_wait_recv(4)
+    y_start(6)
+    backward(1)
+    back(1)
+    y_wait_recv(6)
+    x_start(6)
+    x_to_y(1, 2)
+    x_start(7)
+    x_start(8)
+    weight_grads(1)
+    y_wait_recv(5)
+    y_start(7)
+    backward(2)
+    weight_grads(2)
+    grad_begin()
+    back(2)
+    y_wait_recv(7)
+    x_start(9)
+    x_start(10)
+    y_start(8)
 
     def last_return():
         y_wait_recv(8)
@@ -520,7 +563,7 @@
             jax.ShapeDtypeStruct((NZ, NY, BS // NY, LANES), F32),
             jax.ShapeDtypeStruct((8, LANES), F32),
         ),
-        in_specs=[hbm, hbm] + [vm] * 6,
+        in_specs=[hbm] * 5 + [vm] * 3,
         out_specs=(hbm, vm, vm),
         scratch_shapes=[
             pltpu.VMEM((2, 2, 2, 2, BS, BS), BF16),
@@ -530,15 +573,18 @@
             pltpu.VMEM((1, 2 * CH), F32),
             pltpu.VMEM((4, CH, CH), F32),
             pltpu.VMEM((1, 2 * CH), F32),
-            pltpu.VMEM((NZ, BS + 8, CH), F32),
-            pltpu.VMEM((NZ, BS + 8, CH), F32),
+            pltpu.VMEM((NZ, BS + SUB, CH), BF16),
+            pltpu.VMEM((NZ, BS + SUB, CH), BF16),
             pltpu.VMEM((NY, BS // NY + 8, CH), F32),
             pltpu.VMEM((NY, BS // NY + 8, CH), F32),
             pltpu.VMEM((BS // NY + 8, CH), F32),
             pltpu.VMEM((ND, BS // NY + 8, CH), F32),
             pltpu.VMEM((NY, BS // NY, LANES), F32),
-            pltpu.VMEM((NZ, NY, BS // NY, LANES), F32),
-            pltpu.VMEM((ROWS, HALF, CH), BF16),
+            pltpu.VMEM((BS, LANES), BF16),
+            pltpu.VMEM((NZ, BS, LANES), BF16),
+            pltpu.VMEM((2 * KW, HALF), BF16),
+            pltpu.VMEM((2 * NLAT, 2 * NLAT), BF16),
+            pltpu.VMEM((2 * NLAT, 2 * NLAT), BF16),
             pltpu.VMEM((ROWS, HALF, CH), BF16),
             pltpu.VMEM((3, GH * WAVES, 128), F32),
             pltpu.VMEM((2, NJ, ND, NG, NY, SUB, CH), BF16),
@@ -547,13 +593,15 @@
             pltpu.VMEM((2, NJ, NY, QROWS, CH), BF16),
             pltpu.VMEM((NJ, NY, QROWS, CH), BF16),
             pltpu.VMEM((NJ, NY, QROWS, CH), BF16),
+            pltpu.VMEM((NJ, NLAT, 2 * CH), BF16),
+            pltpu.VMEM((NJ, NLAT, 2 * CH), BF16),
             pltpu.VMEM((NLAT, 2 * CH), BF16),
             pltpu.VMEM((NLAT, 2 * CH), BF16),
-            pltpu.VMEM((NLAT, 2 * CH), BF16),
-            pltpu.VMEM((NLAT, 2 * CH), BF16),
-            pltpu.VMEM((NLAT, 2 * CH), F32),
+            pltpu.VMEM((NJ, NLAT, 2 * CH), F32),
+            pltpu.VMEM((NJ, NLAT, 2 * CH), F32),
             pltpu.VMEM((2 * NLAT, CH), BF16),
             dma((2, NG)),
+            dma((3,)),
             dma((18,)),
             dma((18, ND)),
             dma((18, ND)),

time: 165 us -> 161 us (0.976)
  Pallas kernels: 164 us -> 160 us
    pallas_call x1, Pallas kernels: 152 us -> 149 us  [spectral_call(): pl.pallas_call(spectral_kernel, out_shape=(jax.ShapeDtypeStruct((NG, NJ,...]
where the time goes in v5:
time: 161 us
  Pallas kernels  160 us (99%)
    pallas_call x1, Pallas kernels, spectral_call(): pl.pallas_call(spectral_kernel, out_shape=(jax.ShapeDtypeStruct((NG, NJ,...  149 us
    pallas_call x1, Pallas kernels, inverse_call(): pl.pallas_call(inverse_kernel, out_shape=(jax.ShapeDtypeStruct((1, ROWS,...  11.7 us

profile of v5, /device:TPU:1, one launch (start us, length us, event | category | flops | bytes accessed | tf_op | source)
XLA Modules:
  0.0 161.1 jit_solution(18053576440706877005)
XLA Ops:
  0.6 148.5 %spectral.1 = (bf16[3,3,8,4,16,384]{5,4,3,2,1,0:T(8,128)(2,1)}, f32[4,4,24,256]{3,2,1,0:T(8,128)}, f32[8,256]{1,0:T(8,128)}) custom-call(bf16[1,24,384,384]{3,2,1,0:T(8,128)(2,1)} %f_hbm.1, bf16[1,24,384,384]{3,2,1,0:T(8,128)(2,1)} %cot_hbm.1, bf16[2,192,384]{2,1,0:T(8,128)(2,1)} %constant.8.clone.tw_hbm, bf16[768,768]{1,0:T(8,128)(2,1)} %constant.10.clone.th_hbm, ...), custom_call_target="tpu_custom_call" | custom-call | flops 10000000000 | bytes 30000000 | tf_op jit(solution)/shard_map/spectral/pallas_call | solution.py:559
  149.2 11.7 %inverse.1 = (bf16[1,24,384,384]{3,2,1,0:T(8,128)(2,1)}, f32[2,2,96,96]{3,2,1,0:T(8,128)}, f32[2,2,96,96]{3,2,1,0:T(8,128)}, f32[2,2,96]{2,1,0:T(2,128)}) custom-call(bf16[3,3,8,4,16,384]{5,4,3,2,1,0:T(8,128)(2,1)} %get-tuple-element.7.back_hbm, bf16[1,24,384,384]{3,2,1,0:T(8,128)(2,1)} %cot_hbm.1, bf16[2,384,192]{2,1,0:T(8,128)(2,1)} %constant.9.clone.twt_hbm, ...), custom_call_target="tpu_custom_call" | custom-call | flops 1400000000 | bytes 18000000 | tf_op jit(solution)/shard_map/inverse/pallas_call | solution.py:724

commit v6 on v5

--- a/solution.py
+++ b/solution.py
@@ -659,11 +659,9 @@
         return pltpu.make_async_copy(buf.at[rows], out_hbm.at[0, rows], out_sem.at[i])
 
     table = pltpu.make_async_copy(twt_hbm.at[xhi], twt, twt_sem.at[0])
-    for g in range(NG):
-        load_back(g).start()
-        if g == 0:
-            table.start()
-        load_cot(g).start()
+    load_back(0).start()
+    table.start()
+    load_cot(0).start()
 
     scale = 1.0 / math.sqrt(SPEC_ROWS)
     row = lax.broadcasted_iota(jnp.int32, (LANES, BS), 0)
@@ -685,6 +683,11 @@
     @pl.loop(0, NG)
     def _(g):
         load_back(g).wait()
+
+        @pl.when(g + 1 < NG)
+        def _():
+            load_back(g + 1).start()
+            load_cot(g + 1).start()
 
         @pl.loop(0, NJ * ND)
         def _(jd):

time: 161 us -> 160 us (level)
  no operation moved by 1% of the time
where the time goes in v6:
time: 160 us
  Pallas kernels  159 us (99%)
    pallas_call x1, Pallas kernels, spectral_call(): pl.pallas_call(spectral_kernel, out_shape=(jax.ShapeDtypeStruct((NG, NJ,...  149 us
    pallas_call x1, Pallas kernels, inverse_call(): pl.pallas_call(inverse_kernel, out_shape=(jax.ShapeDtypeStruct((1, ROWS,...  10.4 us

profile of v6, /device:TPU:1, one launch (start us, length us, event | category | flops | bytes accessed | tf_op | source)
XLA Modules:
  0.0 159.7 jit_solution(9279881550975484408)
XLA Ops:
  0.6 148.5 %spectral.1 = (bf16[3,3,8,4,16,384]{5,4,3,2,1,0:T(8,128)(2,1)}, f32[4,4,24,256]{3,2,1,0:T(8,128)}, f32[8,256]{1,0:T(8,128)}) custom-call(bf16[1,24,384,384]{3,2,1,0:T(8,128)(2,1)} %f_hbm.1, bf16[1,24,384,384]{3,2,1,0:T(8,128)(2,1)} %cot_hbm.1, bf16[2,192,384]{2,1,0:T(8,128)(2,1)} %constant.8.clone.tw_hbm, bf16[768,768]{1,0:T(8,128)(2,1)} %constant.10.clone.th_hbm, ...), custom_call_target="tpu_custom_call" | custom-call | flops 10000000000 | bytes 30000000 | tf_op jit(solution)/shard_map/spectral/pallas_call | solution.py:559
  149.2 10.4 %inverse.1 = (bf16[1,24,384,384]{3,2,1,0:T(8,128)(2,1)}, f32[2,2,96,96]{3,2,1,0:T(8,128)}, f32[2,2,96,96]{3,2,1,0:T(8,128)}, f32[2,2,96]{2,1,0:T(2,128)}) custom-call(bf16[3,3,8,4,16,384]{5,4,3,2,1,0:T(8,128)(2,1)} %get-tuple-element.7.back_hbm, bf16[1,24,384,384]{3,2,1,0:T(8,128)(2,1)} %cot_hbm.1, bf16[2,384,192]{2,1,0:T(8,128)(2,1)} %constant.9.clone.twt_hbm, ...), custom_call_target="tpu_custom_call" | custom-call | flops 1400000000 | bytes 18000000 | tf_op jit(solution)/shard_map/inverse/pallas_call | solution.py:727
